TPU v7x, 32 devices: a whole 2x2x4 slice. The times are simulated.
32 devices in a mesh: clip: 8 (over z, y), frame: 4 (over x, core).
Axes of the slice: x: 2, y: 2, z: 4, core: 2. Of those that a mesh axis runs over, the one named last changes fastest.
Arguments:
- clips_in: bfloat16 [8, 8, 20, 20, 320], P('clip', 'frame'), may hold values from -6 to 6
- out_grad: bfloat16 [8, 8, 20, 20, 320], P('clip', 'frame'), may hold values from -6 to 6
- clip_side: int32 [8], P('clip'), may hold values from 14 to 20, as said below
- qkv_weight: float32 [960, 320], P('frame'), may hold values from -0.3125 to 0.3125
- proj_weight: float32 [320, 320], P('frame'), may hold values from -6 to 6
- up_weight: float32 [1280, 320], P('frame'), may hold values from -0.3125 to 0.3125
- down_weight: float32 [1280, 320], P('frame'), may hold values from -0.15625 to 0.15625
- qkv_moment: float32 [960, 320], P('frame'), may hold values from -512 to 512
- proj_moment: float32 [320, 320], P('frame'), may hold values from -512 to 512
- up_moment: float32 [1280, 320], P('frame'), may hold values from -512 to 512
- down_moment: float32 [1280, 320], P('frame'), may hold values from -512 to 512
- vectors: float32 [9, 320], replicated
- vector_mean: float32 [9, 320], replicated, may hold values from -48 to 48
- vector_square: float32 [9, 320], replicated, may hold values from 5.12 to 51.2
- up_bias: float32 [1280], replicated, may hold values from -3 to 3
- up_bias_mean: float32 [1280], replicated, may hold values from -48 to 48
- up_bias_square: float32 [1280], replicated, may hold values from 5.12 to 51.2
- conv_kernel: float32 [27, 320], replicated, may hold values from -1.25 to 1.25
- kernel_mean: float32 [27, 320], replicated, may hold values from -48 to 48
- kernel_square: float32 [27, 320], replicated, may hold values from 5.12 to 51.2
Outputs:
- block_out: bfloat16 [8, 8, 20, 20, 320], P('clip', 'frame')
- input_grad: float32 [8, 8, 20, 20, 320], P('clip', 'frame')
- qkv_moment_new: float32 [960, 320], P('frame')
- qkv_weight_new: float32 [960, 320], P('frame')
- proj_moment_new: float32 [320, 320], P('frame')
- proj_weight_new: float32 [320, 320], P('frame')
- up_moment_new: float32 [1280, 320], P('frame')
- up_weight_new: float32 [1280, 320], P('frame')
- down_moment_new: float32 [1280, 320], P('frame')
- down_weight_new: float32 [1280, 320], P('frame')
- vector_mean_new: float32 [9, 320], replicated
- vector_square_new: float32 [9, 320], replicated
- vectors_new: float32 [9, 320], replicated
- up_bias_mean_new: float32 [1280], replicated
- up_bias_square_new: float32 [1280], replicated
- up_bias_new: float32 [1280], replicated
- kernel_mean_new: float32 [27, 320], replicated
- kernel_square_new: float32 [27, 320], replicated
- kernel_new: float32 [27, 320], replicated
Inputs may be any that keep to these rules, and one draw needn't show every extreme that they name: `clip_side`: each entry is 14 or 20; both occur in every draw.
All inputs are finite; a program needn't handle non-finite values.
Results may differ from a plain program's by a relative error of at most 0.009.
The roundings to bfloat16 on the way count: a program that leaves them out, or rounds other values in their place, can miss the bound.
Values may be sent and summed in bfloat16 or wider, within the bound.
A program may use at most 128 MiB of HBM per device.

v0:
```python
import math

import jax
import jax.numpy as jnp
from jax import lax
from jax.sharding import PartitionSpec as P

D = 320
HEADS = 5
HEAD_DIM = 64
FF = 1280
QBLOCKS = 5
NS_STEPS = 5
STEP = 10
CLIP_TOK = 3200


HIGHEST = lax.Precision.HIGHEST
POLY_ONE = 3.4445
POLY_TWO = -4.775
POLY_THREE = 2.0315


def padded_2(block, sides, width):
    for axis, dim in sides:
        count = lax.axis_size(axis)
        forward = [(i, i + 1) for i in range(count - 1)]
        backward = [(target, source) for source, target in forward]
        low = lax.ppermute(
            lax.slice_in_dim(block, block.shape[dim] - width, None, axis=dim), axis, forward
        )
        high = lax.ppermute(lax.slice_in_dim(block, 0, width, axis=dim), axis, backward)
        block = jnp.concatenate([low, block, high], axis=dim)
    return block


def layer_norm(rows_in, gain_vec, shift_vec):
    average = jnp.mean(rows_in, axis=-1, keepdims=True)
    centered = rows_in - average
    variance = jnp.mean(centered * centered, axis=-1, keepdims=True)
    return centered * lax.rsqrt(variance + 1e-05) * gain_vec + shift_vec


def gelu_exact(values):
    return jax.nn.gelu(values, approximate=False)


def depthwise(padded, conv_kernel, frame_count, grid_side):
    summed = jnp.zeros(
        padded.shape[:-4] + (frame_count, grid_side, grid_side, padded.shape[-1]), jnp.float32
    )
    for offset in range(27):
        depth_at, remain = divmod(offset, 9)
        row_at, column_at = divmod(remain, 3)
        summed = (
            summed
            + conv_kernel[offset]
            * padded[
                ...,
                depth_at : depth_at + frame_count,
                row_at : row_at + grid_side,
                column_at : column_at + grid_side,
                :,
            ]
        )
    return summed


def depthwise_back(up_padded, conv_kernel, frame_count, grid_side):
    summed = jnp.zeros(
        up_padded.shape[:-4] + (frame_count, grid_side, grid_side, up_padded.shape[-1]), jnp.float32
    )
    for offset in range(27):
        depth_at, remain = divmod(offset, 9)
        row_at, column_at = divmod(remain, 3)
        summed = (
            summed
            + conv_kernel[offset]
            * up_padded[
                ...,
                2 - depth_at : 2 - depth_at + frame_count,
                2 - row_at : 2 - row_at + grid_side,
                2 - column_at : 2 - column_at + grid_side,
                :,
            ]
        )
    return summed


def kernel_terms(padded, upstream, frame_count, grid_side):
    pieces = []
    for offset in range(27):
        depth_at, remain = divmod(offset, 9)
        row_at, column_at = divmod(remain, 3)
        window = padded[
            ...,
            depth_at : depth_at + frame_count,
            row_at : row_at + grid_side,
            column_at : column_at + grid_side,
            :,
        ]
        pieces.append(jnp.sum(upstream * window, axis=tuple(range(upstream.ndim - 1))))
    return jnp.stack(pieces)


def self_product(block_in):
    return jnp.dot(block_in.T, block_in, precision=HIGHEST)


def gram_sums(blocks):
    return (
        lax.psum(self_product(blocks[0]).astype(jnp.bfloat16), "frame").astype(jnp.float32),
        lax.psum(self_product(blocks[1]).astype(jnp.bfloat16), "frame").astype(jnp.float32),
        lax.psum(self_product(blocks[2]).astype(jnp.bfloat16), "frame").astype(jnp.float32),
        lax.psum(self_product(blocks[3]).astype(jnp.bfloat16), "frame").astype(jnp.float32),
    )


def poly_step(current, gram_mat):
    return POLY_ONE * current + jnp.dot(
        current,
        POLY_TWO * gram_mat + POLY_THREE * jnp.dot(gram_mat, gram_mat, precision=HIGHEST),
        precision=HIGHEST,
    )


def adamw(param, mean_old, square_old, gradient, rate_value, decay):
    mean_new = 0.9 * mean_old + 0.1 * gradient
    square_new = 0.999 * square_old + 0.001 * gradient * gradient
    mean_hat = mean_new / (1.0 - 0.9**STEP)
    square_hat = square_new / (1.0 - 0.999**STEP)
    return (
        mean_new,
        square_new,
        param - rate_value * (mean_hat / (jnp.sqrt(square_hat) + 1e-08) + decay * param),
    )


def per_device(
    clips_in,
    out_grad,
    clip_side,
    qkv_weight,
    proj_weight,
    up_weight,
    down_weight,
    qkv_moment,
    proj_moment,
    up_moment,
    down_moment,
    vectors,
    vector_mean,
    vector_square,
    up_bias,
    up_bias_mean,
    up_bias_square,
    conv_kernel,
    kernel_mean,
    kernel_square,
):
    clip_count = clips_in.shape[0]
    frame_count = clips_in.shape[1]
    grid_side = clips_in.shape[2]
    frame_devices = lax.axis_size("frame")
    slot_count = 2 * frame_devices
    local_tokens = frame_count * grid_side * grid_side
    clip_tokens = local_tokens * frame_devices
    row_total = clip_count * local_tokens
    block_rows = clip_tokens // QBLOCKS
    score_scale = HEAD_DIM ** (-0.5)
    qkv_full, proj_full, up_full, down_full = (
        lax.all_gather(qkv_weight.astype(jnp.bfloat16), "frame", axis=0, tiled=True),
        lax.all_gather(proj_weight.astype(jnp.bfloat16), "frame", axis=0, tiled=True),
        lax.all_gather(up_weight.astype(jnp.bfloat16), "frame", axis=0, tiled=True),
        lax.all_gather(down_weight.astype(jnp.bfloat16), "frame", axis=0, tiled=True),
    )
    head_ids = jnp.arange(HEADS, dtype=jnp.int32)
    slot_of = jnp.where(head_ids < 2, head_ids, 2 * (head_ids - 1))
    slot_table = (slot_of[:, None] == jnp.arange(slot_count, dtype=jnp.int32)[None, :]).astype(
        jnp.bfloat16
    )
    grid_pos = jnp.arange(grid_side, dtype=jnp.int32)
    limits = clip_side[:, None, None]
    inside = (grid_pos[None, :, None] < limits) & (grid_pos[None, None, :] < limits)
    inside_cells = inside.astype(jnp.float32)[:, None, :, :, None]
    key_ok = jnp.broadcast_to(
        inside[:, None], (clip_count, frame_count * frame_devices, grid_side, grid_side)
    ).reshape(clip_count, clip_tokens)
    masked = clips_in * inside_cells.astype(jnp.bfloat16)
    rimmed = padded_2(masked, (("frame", 1),), 1)
    padded = jnp.pad(rimmed.astype(jnp.float32), ((0, 0), (0, 0), (1, 1), (1, 1), (0, 0)))
    first_res = (
        clips_in.astype(jnp.float32)
        + depthwise(padded, conv_kernel, frame_count, grid_side)
        + vectors[4]
    )
    tokens = first_res.reshape(row_total, D)
    normed = layer_norm(tokens, vectors[0], vectors[1]).astype(jnp.bfloat16)
    qkv_bias = jnp.concatenate([vectors[5], jnp.zeros((D,), jnp.float32), vectors[6]])
    joined = (
        jnp.einsum("tc,oc->to", normed, qkv_full, preferred_element_type=jnp.float32) + qkv_bias
    ).astype(jnp.bfloat16)
    slotted = jnp.einsum(
        "tkhd,hs->tksd",
        joined.reshape(row_total, 3, HEADS, HEAD_DIM),
        slot_table,
        preferred_element_type=jnp.float32,
    ).astype(jnp.bfloat16)
    heads_in = lax.all_to_all(
        slotted.reshape(clip_count, local_tokens, 3, slot_count * HEAD_DIM),
        "frame",
        split_axis=3,
        concat_axis=1,
        tiled=True,
    )
    per_slot = jnp.moveaxis(heads_in.reshape(clip_count, clip_tokens, 3, 2, HEAD_DIM), 3, 0)
    queries = per_slot[:, :, :, 0]
    key_rows = per_slot[:, :, :, 1]
    values = per_slot[:, :, :, 2]

    def split_blocks(slot_array):
        return jnp.moveaxis(
            slot_array.reshape(clip_count, QBLOCKS, block_rows, slot_array.shape[-1]), 1, 0
        )

    def slot_scores(query_block, slot_keys):
        scores = (
            jnp.einsum("cqd,ckd->cqk", query_block, slot_keys, preferred_element_type=jnp.float32)
            * score_scale
        )
        return jnp.where(key_ok[:, None, :], scores, -1e30)

    def slot_forward(operands):
        slot_queries, slot_keys, slot_values = operands

        def block_forward(query_block):
            scores = slot_scores(query_block, slot_keys)
            row_peak = jnp.max(scores, axis=-1, keepdims=True)
            exp_terms = jnp.exp(scores - row_peak)
            totals = jnp.sum(exp_terms, axis=-1, keepdims=True)
            attn_probs = (exp_terms / totals).astype(jnp.bfloat16)
            mixed_out = jnp.einsum(
                "cqk,ckd->cqd", attn_probs, slot_values, preferred_element_type=jnp.float32
            )
            return (mixed_out.astype(jnp.bfloat16), row_peak[..., 0] + jnp.log(totals[..., 0]))

        return lax.map(block_forward, split_blocks(slot_queries))

    mixed_all, log_sums = lax.map(slot_forward, (queries, key_rows, values))
    attended_heads = jnp.transpose(mixed_all, (2, 1, 3, 0, 4)).reshape(
        clip_count, clip_tokens, 2 * HEAD_DIM
    )
    attended_slots = lax.all_to_all(
        attended_heads, "frame", split_axis=1, concat_axis=2, tiled=True
    )
    attended = (
        jnp.einsum(
            "tsd,hs->thd",
            attended_slots.reshape(row_total, slot_count, HEAD_DIM),
            slot_table,
            preferred_element_type=jnp.float32,
        )
        .astype(jnp.bfloat16)
        .reshape(row_total, D)
    )
    branch = (
        jnp.einsum("tc,oc->to", attended, proj_full, preferred_element_type=jnp.float32)
        + vectors[7]
    )
    second = tokens + branch
    normed_two = layer_norm(second, vectors[2], vectors[3]).astype(jnp.bfloat16)
    hidden = (
        jnp.einsum("tc,hc->th", normed_two, up_full, preferred_element_type=jnp.float32) + up_bias
    )
    activated = gelu_exact(hidden).astype(jnp.bfloat16)
    output = jnp.dot(activated, down_full, preferred_element_type=jnp.float32) + vectors[8]
    block_out = (second + output).reshape(clips_in.shape).astype(jnp.bfloat16)
    grad_top = (out_grad.astype(jnp.float32) * inside_cells).reshape(row_total, D)
    top_low = grad_top.astype(jnp.bfloat16)
    grad_down = jnp.einsum("th,tc->hc", activated, top_low, preferred_element_type=jnp.float32)
    grad_act = jnp.einsum("tc,hc->th", top_low, down_full, preferred_element_type=jnp.float32)
    gelu_value, gelu_back = jax.vjp(gelu_exact, hidden)
    grad_hidden = gelu_back(grad_act)[0].astype(jnp.bfloat16)
    grad_up = jnp.einsum("th,tc->hc", grad_hidden, normed_two, preferred_element_type=jnp.float32)
    grad_normed_two = jnp.dot(grad_hidden, up_full, preferred_element_type=jnp.float32)
    norm_value, norm_back = jax.vjp(layer_norm, second, vectors[2], vectors[3])
    back_second, grad_gain_two, grad_shift_two = norm_back(grad_normed_two)
    grad_second = grad_top + back_second
    branch_low = grad_second.astype(jnp.bfloat16)
    grad_proj = jnp.einsum("to,tc->oc", branch_low, attended, preferred_element_type=jnp.float32)
    grad_attended = jnp.dot(branch_low, proj_full, preferred_element_type=jnp.float32).astype(
        jnp.bfloat16
    )
    grad_slots = jnp.einsum(
        "thd,hs->tsd",
        grad_attended.reshape(row_total, HEADS, HEAD_DIM),
        slot_table,
        preferred_element_type=jnp.float32,
    ).astype(jnp.bfloat16)
    grad_heads = lax.all_to_all(
        grad_slots.reshape(clip_count, local_tokens, slot_count * HEAD_DIM),
        "frame",
        split_axis=2,
        concat_axis=1,
        tiled=True,
    )
    grad_mixed = jnp.moveaxis(grad_heads.reshape(clip_count, clip_tokens, 2, HEAD_DIM), 2, 0)

    def slot_backward(operands):
        slot_queries, slot_keys, slot_values, slot_grads, slot_logsum = operands

        def block_backward(running, block_in):
            key_acc, value_acc = running
            query_block, grad_block, logsum_block = block_in
            scores = slot_scores(query_block, slot_keys)
            attn_probs = jnp.exp(scores - logsum_block[..., None])
            grad_probs = jnp.einsum(
                "cqd,ckd->cqk", grad_block, slot_values, preferred_element_type=jnp.float32
            )
            row_dot = jnp.sum(attn_probs * grad_probs, axis=-1, keepdims=True)
            grad_scores = (attn_probs * (grad_probs - row_dot)).astype(jnp.bfloat16)
            grad_query = (
                jnp.einsum(
                    "cqk,ckd->cqd", grad_scores, slot_keys, preferred_element_type=jnp.float32
                )
                * score_scale
            )
            key_acc = (
                key_acc
                + jnp.einsum(
                    "cqk,cqd->ckd", grad_scores, query_block, preferred_element_type=jnp.float32
                )
                * score_scale
            )
            value_acc = value_acc + jnp.einsum(
                "cqk,cqd->ckd",
                attn_probs.astype(jnp.bfloat16),
                grad_block,
                preferred_element_type=jnp.float32,
            )
            return ((key_acc, value_acc), grad_query)

        zero_acc = jnp.zeros(slot_keys.shape, jnp.float32)
        sums_out, query_grad = lax.scan(
            block_backward,
            (zero_acc, zero_acc),
            (split_blocks(slot_queries), split_blocks(slot_grads), slot_logsum),
        )
        return (query_grad, sums_out[0], sums_out[1])

    query_grad, key_grad, value_grad = lax.map(
        slot_backward, (queries, key_rows, values, grad_mixed, log_sums)
    )
    query_part = jnp.transpose(query_grad, (2, 1, 3, 0, 4)).reshape(
        clip_count, clip_tokens, 2, HEAD_DIM
    )
    key_part = jnp.transpose(key_grad, (1, 2, 0, 3))
    value_part = jnp.transpose(value_grad, (1, 2, 0, 3))
    grad_joined_heads = (
        jnp.stack([query_part, key_part, value_part], axis=2)
        .astype(jnp.bfloat16)
        .reshape(clip_count, clip_tokens, 3, 2 * HEAD_DIM)
    )
    back_slots = lax.all_to_all(grad_joined_heads, "frame", split_axis=1, concat_axis=3, tiled=True)
    grad_joined = (
        jnp.einsum(
            "tksd,hs->tkhd",
            back_slots.reshape(row_total, 3, slot_count, HEAD_DIM),
            slot_table,
            preferred_element_type=jnp.float32,
        )
        .astype(jnp.bfloat16)
        .reshape(row_total, 3 * D)
    )
    grad_qkv = jnp.einsum("to,tc->oc", grad_joined, normed, preferred_element_type=jnp.float32)
    grad_query_bias = jnp.sum(grad_joined[:, :D], axis=0, dtype=jnp.float32)
    grad_value_bias = jnp.sum(grad_joined[:, 2 * D :], axis=0, dtype=jnp.float32)
    grad_normed = jnp.dot(grad_joined, qkv_full, preferred_element_type=jnp.float32)
    first_value, first_back = jax.vjp(layer_norm, tokens, vectors[0], vectors[1])
    back_first, grad_gain_one, grad_shift_one = first_back(grad_normed)
    grad_first = grad_second + back_first
    grad_cells = grad_first.reshape(clip_count, frame_count, grid_side, grid_side, D)
    grad_rims = padded_2(grad_cells.astype(jnp.bfloat16), (("frame", 1),), 1).astype(
        grad_cells.dtype
    )
    up_padded = jnp.pad(grad_rims, ((0, 0), (0, 0), (1, 1), (1, 1), (0, 0)))
    input_grad = (
        grad_cells + depthwise_back(up_padded, conv_kernel, frame_count, grid_side) * inside_cells
    )
    kernel_grad = kernel_terms(padded, grad_cells, frame_count, grid_side)
    vector_grad = jnp.stack(
        [
            grad_gain_one,
            grad_shift_one,
            grad_gain_two,
            grad_shift_two,
            jnp.sum(grad_first, axis=0),
            grad_query_bias,
            grad_value_bias,
            jnp.sum(branch_low, axis=0, dtype=jnp.float32),
            jnp.sum(top_low, axis=0, dtype=jnp.float32),
        ]
    )
    up_bias_grad = jnp.sum(grad_hidden, axis=0, dtype=jnp.float32)
    vector_total, bias_total, kernel_total = lax.psum(
        (vector_grad, up_bias_grad, kernel_grad), ("clip", "frame")
    )
    summed_full = lax.psum((grad_qkv, grad_proj, grad_up, grad_down), "clip")
    shares = (
        lax.psum_scatter(
            summed_full[0].astype(jnp.bfloat16), "frame", scatter_dimension=0, tiled=True
        ).astype(jnp.float32),
        lax.psum_scatter(
            summed_full[1].astype(jnp.bfloat16), "frame", scatter_dimension=0, tiled=True
        ).astype(jnp.float32),
        lax.psum_scatter(
            summed_full[2].astype(jnp.bfloat16), "frame", scatter_dimension=0, tiled=True
        ).astype(jnp.float32),
        lax.psum_scatter(
            summed_full[3].astype(jnp.bfloat16), "frame", scatter_dimension=0, tiled=True
        ).astype(jnp.float32),
    )
    moments = (
        0.95 * qkv_moment + shares[0],
        0.95 * proj_moment + shares[1],
        0.95 * up_moment + shares[2],
        0.95 * down_moment + shares[3],
    )
    squares = lax.psum(
        (
            jnp.sum(moments[0] * moments[0]),
            jnp.sum(moments[1] * moments[1]),
            jnp.sum(moments[2] * moments[2]),
            jnp.sum(moments[3] * moments[3]),
        ),
        "frame",
    )
    scaled = [moments[which] / (jnp.sqrt(squares[which]) + 1e-07) for which in range(4)]
    for rounds in range(NS_STEPS):
        gram_mats = gram_sums(scaled)
        scaled = [poly_step(scaled[which], gram_mats[which]) for which in range(4)]
    qkv_new = 0.999 * qkv_weight - 0.2 * math.sqrt(3.0) * scaled[0]
    proj_new = 0.999 * proj_weight - 0.12 * math.sqrt(CLIP_TOK) * scaled[1]
    up_new = 0.999 * up_weight - 0.2 * math.sqrt(FF / D) * scaled[2]
    down_new = 0.999 * down_weight - 0.2 * scaled[3]
    vec_mean, vec_square, vec_new = adamw(
        vectors, vector_mean, vector_square, vector_total, 0.2, 0.0
    )
    bias_mean, bias_square, bias_new = adamw(
        up_bias, up_bias_mean, up_bias_square, bias_total, 0.2, 0.0
    )
    kern_mean, kern_square, kern_new = adamw(
        conv_kernel, kernel_mean, kernel_square, kernel_total, 0.05, 0.01
    )
    return (
        block_out,
        input_grad,
        moments[0],
        qkv_new,
        moments[1],
        proj_new,
        moments[2],
        up_new,
        moments[3],
        down_new,
        vec_mean,
        vec_square,
        vec_new,
        bias_mean,
        bias_square,
        bias_new,
        kern_mean,
        kern_square,
        kern_new,
    )


def solution(mesh):
    placed = (
        P("clip", "frame", None, None, None),
        P("clip", "frame", None, None, None),
        P("clip"),
        P("frame", None),
        P("frame", None),
        P("frame", None),
        P("frame", None),
        P("frame", None),
        P("frame", None),
        P("frame", None),
        P("frame", None),
        P(),
        P(),
        P(),
        P(),
        P(),
        P(),
        P(),
        P(),
        P(),
    )
    return jax.shard_map(
        per_device,
        mesh=mesh,
        in_specs=placed,
        out_specs=(
            P("clip", "frame", None, None, None),
            P("clip", "frame", None, None, None),
            P("frame", None),
            P("frame", None),
            P("frame", None),
            P("frame", None),
            P("frame", None),
            P("frame", None),
            P("frame", None),
            P("frame", None),
            P(),
            P(),
            P(),
            P(),
            P(),
            P(),
            P(),
            P(),
            P(),
        ),
        check_vma=False,
    )
```

profile of v0, /device:TPU:1, one launch (start us, length us, event | category | flops | bytes accessed | tf_op | source)
XLA Modules:
  0.0 1218.1 jit_solution(17153710172984550679)
XLA Ops:
  10.1 4.5 collective-permute-start
  17.1 11.2 all-gather
  31.0 7.1 fusion.172
  54.6 5.0 all-to-all-start
  63.4 41.1 %all_gather.13 = bf16[320,320]{1,0:T(8,128)(2,1)} all-gather(bf16[80,320]{1,0:T(8,128)(2,1)S(1)} %convert_element_type.353), channel_id=1, replica_groups=mesh['clip'=8,'frame'=4] {'frame'}, dimensions={0}, use_global_device_ids=true | all-gather | bytes 256000 | tf_op jit(solution)/shard_map/all_gather | solution.py:173
  104.5 6.7 copy.242
  111.3 5.4 copy.205
  126.5 53.7 %while.60 = (s32[]{:T(128)}, bf16[2,5,1,640,64]{3,4,1,2,0:T(8,128)(2,1)}, f32[2,5,1,640]{3,2,1,0:T(1,128)S(1)}, bf16[2,1,3200,64]{3,2,1,0:T(8,128)(2,1)}, bf16[2...) while((s32[]{:T(128)}, ...), condition=%wide.region_7.8_spmd.clone, body=%wide.region_2.7_spmd.clone.sunk | while | flops 540712320 | bytes 29820008 | solution.py:249
  129.4 23.1 %while.63 = (s32[]{:T(128)}, bf16[5,1,640,64]{2,3,1,0:T(8,128)(2,1)S(1)}, f32[5,1,640]{2,1,0:T(1,128)S(1)}, pred[1,8,20,20]{3,2,1,0:T(8,128)(4,1)}, bf16[5,1,640...) while((s32[]{:T(128)}, ...), condition=%wide.wide.region_6.6_spmd, body=%wide.wide.region_3.5_spmd.sunk | while | flops 540712320 | bytes 26494576 | solution.py:247
  156.2 23.1 %while.63 = (s32[]{:T(128)}, bf16[5,1,640,64]{2,3,1,0:T(8,128)(2,1)S(1)}, f32[5,1,640]{2,1,0:T(1,128)S(1)}, pred[1,8,20,20]{3,2,1,0:T(8,128)(4,1)}, bf16[5,1,640...) while((s32[]{:T(128)}, ...), condition=%wide.wide.region_6.6_spmd, body=%wide.wide.region_3.5_spmd.sunk | while | flops 540712320 | bytes 26494576 | solution.py:247
  185.1 17.6 %reduce.83 = bf16[3200,128]{1,0:T(8,128)(2,1)S(1)} reduce(bf16[3200,1,128]{2,1,0:T(2,128)(2,1)S(1)} %bitcast.358, bf16[]{:T(256)} %broadcast.655), dimensions={1}, to_apply=%bitcast.134.reduce_sub_computation | reduce | bytes 1638402
  207.6 18.0 %all_gather.15 = bf16[1280,320]{1,0:T(8,128)(2,1)S(1)} all-gather(bf16[320,320]{1,0:T(8,128)(2,1)S(1)} %copy-done.52), channel_id=1, replica_groups=mesh['clip'=8,'frame'=4] {'frame'}, dimensions={0}, use_global_device_ids=true | all-gather | bytes 1024000 | tf_op jit(solution)/shard_map/all_gather | solution.py:175
  225.6 10.2 all_gather.14
  240.0 10.8 multiply_convert_fusion.1
  260.9 6.5 reduce.84
  273.9 11.1 all-to-all-done.2
  290.6 250.5 %while.62 = (s32[]{:T(128)}, bf16[2,5,1,640,64]{3,4,1,2,0:T(8,128)(2,1)}, bf16[2,1,3200,64]{2,3,1,0:T(8,128)(2,1)}, bf16[2,1,3200,64]{2,3,1,0:T(8,128)(2,1)}, bf...) while((s32[]{:T(128)}, ...), condition=%wide.region_16.17_spmd.clone, body=%wide.region_12.16_spmd.clone.sunk | while | flops 1330216320 | bytes 118439424 | solution.py:351
  297.5 115.1 %while.64 = (s32[]{:T(128)}, f32[1,3200,64]{1,2,0:T(8,128)S(1)}, f32[1,3200,64]{1,2,0:T(8,128)S(1)}, bf16[5,1,640,64]{2,3,1,0:T(8,128)(2,1)}, pred[1,8,20,20]{3,...) while((s32[]{:T(128)}, f32[1,3200,64]{1,2,0:T(8,128)S(1)}, ...), condition=%wide.wide.region_15.15_spmd.clone, body=%wide.wide.region_13.14_spmd.clone.sunk | while | flops 1330216320 | bytes 103645064 | solution.py:344
  300.0 6.0 multiply_reduce_fusion.40
  306.0 6.8 multiply_convert_fusion.4
  312.8 4.3 fusion.350
  323.0 6.0 multiply_reduce_fusion.40
  329.0 6.8 multiply_convert_fusion.4
  346.0 6.0 multiply_reduce_fusion.40
  352.0 6.8 multiply_convert_fusion.4
  358.8 4.3 fusion.350
  369.1 6.0 multiply_reduce_fusion.40
  375.1 6.8 multiply_convert_fusion.4
  381.8 4.3 fusion.350
  392.1 6.0 multiply_reduce_fusion.40
  398.1 6.8 multiply_convert_fusion.4
  404.9 4.3 fusion.350
  422.7 115.1 %while.64 = (s32[]{:T(128)}, f32[1,3200,64]{1,2,0:T(8,128)S(1)}, f32[1,3200,64]{1,2,0:T(8,128)S(1)}, bf16[5,1,640,64]{2,3,1,0:T(8,128)(2,1)}, pred[1,8,20,20]{3,...) while((s32[]{:T(128)}, f32[1,3200,64]{1,2,0:T(8,128)S(1)}, ...), condition=%wide.wide.region_15.15_spmd.clone, body=%wide.wide.region_13.14_spmd.clone.sunk | while | flops 1330216320 | bytes 103645064 | solution.py:344
  425.2 6.0 multiply_reduce_fusion.40
  431.2 6.8 multiply_convert_fusion.4
  438.0 4.3 fusion.350
  448.2 6.0 multiply_reduce_fusion.40
  454.2 6.8 multiply_convert_fusion.4
  461.0 4.3 fusion.350
  471.3 6.0 multiply_reduce_fusion.40
  477.3 6.8 multiply_convert_fusion.4
  484.1 4.3 fusion.350
  494.3 6.0 multiply_reduce_fusion.40
  500.3 6.8 multiply_convert_fusion.4
  507.1 4.3 fusion.350
  517.3 6.0 multiply_reduce_fusion.40
  523.3 6.8 multiply_convert_fusion.4
  530.1 4.3 fusion.350
  545.5 4.3 copy.229
  549.9 5.6 all-to-all-start.3
  557.2 4.5 fusion.142
  565.3 27.8 %all-to-all-done.3 = bf16[1,3200,3,128]{3,2,0,1:T(4,128)(2,1)} async-done(((bf16[1,3200,3,128]{3,2,0,1:T(4,128)(2,1)}), bf16[1,3200,3,128]{3,2,0,1:T(4,128)(2,1)}, u32[]{:S(2)}, u32[]{:S(2)}) %all-to-all-start.3) | async-done | bytes 2457632 | tf_op jit(solution)/shard_map/all_to_all | solution.py:364
  605.0 226.8 %all-reduce.26 = (bf16[960,320]{0,1:T(8,128)(2,1)}, bf16[320,320]{1,0:T(8,128)(2,1)}, bf16[1280,320]{1,0:T(8,128)(2,1)}, bf16[1280,320]{1,0:T(8,128)(2,1)}) all-reduce(f32[960,320]{0,1:T(8,128)} %fusion.177, f32[320,320]{1,0:T(8,128)S(1)} %fusion.178, f32[1280,320]{1,0:T(8,128)} %fusion.163, ...), channel_id=1, replica_groups=mesh['clip'=8,'frame'=4] {'clip'}, use_global_device_ids=true, to_apply=%region_19.20 | all-reduce | flops 1228800 | bytes 7372800 | tf_op jit(solution)/shard_map/psum | solution.py:408
  857.9 6.7 multiply_reduce_fusion.1
  866.7 8.6 reduce-scatter.13.cloned.1.call-done
  877.7 24.7 %reduce-scatter.11.cloned.1.call-done = bf16[320,320]{1,0:T(8,128)(2,1)} async-done(((bf16[1280,320]{1,0:T(8,128)(2,1)}), bf16[320,320]{1,0:T(8,128)(2,1)}) %reduce-scatter.11.cloned.1.call-update) | async-done | bytes 204816 | tf_op jit(solution)/shard_map/reduce_scatter | solution.py:419
  905.0 24.5 %reduce-scatter.9.cloned.1.call-done = bf16[320,320]{1,0:T(8,128)(2,1)} async-done(((bf16[1280,320]{1,0:T(8,128)(2,1)}), bf16[320,320]{1,0:T(8,128)(2,1)}) %reduce-scatter.9.cloned.1.call-update) | async-done | bytes 204816 | tf_op jit(solution)/shard_map/reduce_scatter | solution.py:416
  931.9 6.4 all-reduce.4
  953.5 33.2 %all-reduce.25.cloned.1.call-done = (bf16[320,320]{1,0:T(8,128)(2,1)}, bf16[320,320]{1,0:T(8,128)(2,1)}, bf16[320,320]{1,0:T(8,128)(2,1)}, bf16[320,320]{1,0:T(8,128)(2,1)}) async-done(((bf16[320,320]{1,0:T(8,128)(2,1)}, bf16[320,320]{1,0:T(8,128)(2,1)}, bf16[320,320]{1,0:T(8,128)(2,1)}, bf16[320,320]{1,0:T(8,128)(2,1)}), (bf16[320,320]{1,0:T(8,128)(2,1)}, bf16[320,320]{1,0:T(8,128)(2,1)}, ...) | async-done | bytes 819216 | tf_op jit(solution)/shard_map/psum | solution.py:112
  1009.1 44.3 %all-reduce.2 = (f32[9,320]{1,0:T(8,128)S(1)}, f32[1280]{0:T(1024)S(1)}, f32[27,320]{1,0:T(8,128)S(1)}) all-reduce(f32[9,320]{1,0:T(8,128)S(1)} %stack.126, f32[1280]{0:T(1024)S(1)} %copy-done.171, f32[27,320]{1,0:T(8,128)S(1)} %stack.154), channel_id=1, replica_groups=mesh['clip'=8,'frame'=4] {'clip','frame'}, use_global_device_ids=true, to_apply=%region_64.65 | all-reduce | flops 12800 | bytes 102400 | tf_op jit(solution)/shard_map/psum | solution.py:405
  1068.0 34.1 %all-reduce.21.cloned.1.call-done = (bf16[320,320]{1,0:T(8,128)(2,1)}, bf16[320,320]{1,0:T(8,128)(2,1)}, bf16[320,320]{1,0:T(8,128)(2,1)}, bf16[320,320]{1,0:T(8,128)(2,1)}) async-done(((bf16[320,320]{1,0:T(8,128)(2,1)}, bf16[320,320]{1,0:T(8,128)(2,1)}, bf16[320,320]{1,0:T(8,128)(2,1)}, bf16[320,320]{1,0:T(8,128)(2,1)}), (bf16[320,320]{1,0:T(8,128)(2,1)}, bf16[320,320]{1,0:T(8,128)(2,1)}, ...) | async-done | bytes 819216 | tf_op jit(solution)/shard_map/psum | solution.py:112
  1117.6 33.8 %all-reduce.19.cloned.1.call-done = (bf16[320,320]{1,0:T(8,128)(2,1)}, bf16[320,320]{1,0:T(8,128)(2,1)}, bf16[320,320]{1,0:T(8,128)(2,1)}, bf16[320,320]{1,0:T(8,128)(2,1)}) async-done(((bf16[320,320]{1,0:T(8,128)(2,1)}, bf16[320,320]{1,0:T(8,128)(2,1)}, bf16[320,320]{1,0:T(8,128)(2,1)}, bf16[320,320]{1,0:T(8,128)(2,1)}), (bf16[320,320]{1,0:T(8,128)(2,1)}, bf16[320,320]{1,0:T(8,128)(2,1)}, ...) | async-done | bytes 819216 | tf_op jit(solution)/shard_map/psum | solution.py:112
  1165.6 8.9 fusion.98
  1177.9 23.9 %all-reduce.17.cloned.1.call-done = (bf16[320,320]{1,0:T(8,128)(2,1)}, bf16[320,320]{1,0:T(8,128)(2,1)}, bf16[320,320]{1,0:T(8,128)(2,1)}, bf16[320,320]{1,0:T(8,128)(2,1)}) async-done(((bf16[320,320]{1,0:T(8,128)(2,1)}, bf16[320,320]{1,0:T(8,128)(2,1)}, bf16[320,320]{1,0:T(8,128)(2,1)}, bf16[320,320]{1,0:T(8,128)(2,1)}), (bf16[320,320]{1,0:T(8,128)(2,1)}, bf16[320,320]{1,0:T(8,128)(2,1)}, ...) | async-done | bytes 819216 | tf_op jit(solution)/shard_map/psum | solution.py:112
  (806 shorter events, 356.3 us)
Async XLA Ops:
  7.2 9.3 copy-start.91
  7.2 9.9 copy-start.49
  8.0 53.0 %copy-start.88 = (f32[20,20]{1,0:T(8,128)}, f32[20,20]{1,0:T(8,128)S(1)}, u32[]{:S(2)}) copy-start(f32[20,20]{1,0:T(8,128)S(1)} %get-tuple-element.677) | copy-start | bytes 4804
  10.1 19.9 %collective-permute-start = (bf16[1,1,20,20,320]{4,3,2,1,0:T(8,128)(2,1)}, bf16[1,1,20,20,320]{4,3,2,1,0:T(8,128)(2,1)S(1)}, u32[]{:S(2)}, u32[]{:S(2)}) collective-permute-start(bf16[1,1,20,20,320]{4,3,2,1,0:T(8,128)(2,1)} %get-tuple-element.671), channel_id=1, source_target_pairs={{0,1},{1,2},{2,3},{4,5},{5,6},{6,7},{8,9},{9,10},{10,11},{12,13},{... | collective-permute-start | bytes 768008 | tf_op jit(solution)/shard_map/ppermute | solution.py:29
  14.6 15.4 %collective-permute-start.1 = (bf16[1,1,20,20,320]{4,3,2,1,0:T(8,128)(2,1)S(1)}, bf16[1,1,20,20,320]{4,3,2,1,0:T(8,128)(2,1)S(1)}, u32[]{:S(2)}, u32[]{:S(2)}) collective-permute-start(bf16[1,1,20,20,320]{4,3,2,1,0:T(8,128)(2,1)S(1)} %get-tuple-element.672), channel_id=1, source_target_pairs={{1,0},{2,1},{3,2},{5,4},{6,5},{7,6},{9,8},{10,9},{11,10},{13,12},{... | collective-permute-start | bytes 768008 | tf_op jit(solution)/shard_map/ppermute | solution.py:32
  17.1 23.7 %copy-start.105 = (f32[320]{0:T(512)}, f32[320]{0:T(512)S(1)}, u32[]{:S(2)}) copy-start(f32[320]{0:T(512)S(1)} %get-tuple-element.529) | copy-start | bytes 3844
  17.1 23.7 %copy-start.172 = (f32[320]{0:T(512)}, f32[320]{0:T(512)S(1)}, u32[]{:S(2)}) copy-start(f32[320]{0:T(512)S(1)} %get-tuple-element.528) | copy-start | bytes 3844
  28.4 17.8 %copy-start.175 = (s32[5]{0:T(128)}, s32[5]{0:T(128)S(1)}, u32[]{:S(2)}) copy-start(s32[5]{0:T(128)S(1)} %compare_select_fusion) | copy-start | bytes 64
  29.5 11.4 copy-start.70
  30.3 7.7 copy-start.1
  54.5 5.0 copy-start.78
  54.5 5.0 copy-start.45
  54.5 5.7 copy-start.47
  54.6 50.0 %all-to-all-start = ((bf16[1,800,3,512]{1,2,0,3:T(4,128)(2,1)}), bf16[1,800,3,512]{1,2,0,3:T(4,128)(2,1)}, u32[]{:S(2)}, u32[]{:S(2)}) async-start(bf16[1,800,3,512]{1,2,0,3:T(4,128)(2,1)} %copy.203), calls=%async_computation | async-start | bytes 7340032 | tf_op jit(solution)/shard_map/all_to_all | solution.py:209
  62.0 49.3 %copy-start.32 = (f32[800,320]{1,0:T(8,128)}, f32[800,320]{1,0:T(8,128)S(1)}, u32[]{:S(2)}) copy-start(f32[800,320]{1,0:T(8,128)S(1)} %reshape.723) | copy-start | bytes 3072004
  202.7 4.8 copy-start.52
  203.8 21.8 %copy-start.51 = (bf16[320,320]{1,0:T(8,128)(2,1)S(1)}, bf16[320,320]{1,0:T(8,128)(2,1)}, u32[]{:S(2)}) copy-start(bf16[320,320]{1,0:T(8,128)(2,1)} %convert_element_type.355) | copy-start | bytes 614404
  203.8 32.0 %all-to-all-start.1 = ((bf16[4,2,51200]{2,1,0:T(2,128)(2,1)}), bf16[4,2,51200]{2,1,0:T(2,128)(2,1)S(1)}, u32[]{:S(2)}, u32[]{:S(2)}) async-start(bf16[4,2,51200]{2,1,0:T(2,128)(2,1)} %reshape.788), calls=%async_computation.1 | async-start | bytes 1638400 | tf_op jit(solution)/shard_map/all_to_all | solution.py:253
  225.6 25.3 %copy-start.53 = (bf16[1280,320]{1,0:T(8,128)(2,1)}, bf16[1280,320]{1,0:T(8,128)(2,1)S(1)}, u32[]{:S(2)}) copy-start(bf16[1280,320]{1,0:T(8,128)(2,1)S(1)} %all_gather.15) | copy-start | bytes 2457604
  239.3 16.7 %copy-start.13 = (f32[800,320]{0,1:T(8,128)}, f32[800,320]{0,1:T(8,128)S(1)}, u32[]{:S(2)}) copy-start(f32[800,320]{0,1:T(8,128)S(1)} %get-tuple-element.681) | copy-start | bytes 3072004
  239.3 16.7 %copy-start.95 = (f32[800]{0:T(1024)}, f32[800]{0:T(1024)S(1)}, u32[]{:S(2)}) copy-start(f32[800]{0:T(1024)S(1)} %broadcast_multiply_fusion.1) | copy-start | bytes 9604
  239.5 16.5 %copy-start.161 = (f32[800]{0:T(1024)}, f32[800]{0:T(1024)S(1)}, u32[]{:S(2)}) copy-start(f32[800]{0:T(1024)S(1)} %fusion.154) | copy-start | bytes 9604
  240.0 10.9 copy-start.33
  270.3 14.8 %all-to-all-start.2 = ((bf16[4,2,51200]{2,1,0:T(2,128)(2,1)}), bf16[4,2,51200]{2,1,0:T(2,128)(2,1)S(1)}, u32[]{:S(2)}, u32[]{:S(2)}) async-start(bf16[4,2,51200]{2,1,0:T(2,128)(2,1)} %reshape.790), calls=%async_computation.2 | async-start | bytes 1638400 | tf_op jit(solution)/shard_map/all_to_all | solution.py:300
  300.0 6.0 copy-start
  323.0 6.0 copy-start
  346.0 6.0 copy-start
  369.1 6.0 copy-start
  392.1 6.0 copy-start
  425.2 6.0 copy-start
  448.2 6.0 copy-start
  471.3 6.0 copy-start
  494.3 6.0 copy-start
  517.3 6.0 copy-start
  549.8 5.8 copy-start.4
  549.8 5.9 copy-start.81
  549.8 5.9 copy-start.90
  549.8 5.9 copy-start.106
  549.9 5.9 copy-start.173
  549.9 43.2 %all-to-all-start.3 = ((bf16[1,3200,3,128]{3,2,0,1:T(4,128)(2,1)}), bf16[1,3200,3,128]{3,2,0,1:T(4,128)(2,1)}, u32[]{:S(2)}, u32[]{:S(2)}) async-start(bf16[1,3200,3,128]{3,2,0,1:T(4,128)(2,1)} %copy.229), calls=%async_computation.3 | async-start | bytes 6553600 | tf_op jit(solution)/shard_map/all_to_all | solution.py:364
  555.5 309.1 %reduce-scatter.7.cloned.1.call-start = ((), (), s32[]{:S(2)}) async-start(), calls=%async_computation.8 | async-start | bytes 307200 | tf_op jit(solution)/shard_map/reduce_scatter | solution.py:413
  557.2 4.6 copy-start.96
  557.2 4.6 copy-start.162
  557.2 4.6 copy-start.164
  602.2 241.8 %copy-start.35 = (bf16[800,3,5,64]{0,3,2,1:T(8,128)(2,1)}, bf16[800,3,5,64]{0,3,2,1:T(8,128)(2,1)S(1)}, u32[]{:S(2)}) copy-start(bf16[800,3,5,64]{0,3,2,1:T(8,128)(2,1)S(1)} %copy.233) | copy-start | bytes 4608004
  831.8 43.5 %reduce-scatter.13.cloned.1.call-start = ((), (), s32[]{:S(2)}) async-start(), calls=%async_computation.11 | async-start | bytes 921600
  834.3 68.1 %reduce-scatter.11.cloned.1.call-start = ((), (), s32[]{:S(2)}) async-start(), calls=%async_computation.10 | async-start | bytes 1228800 | tf_op jit(solution)/shard_map/reduce_scatter | solution.py:419
  835.0 94.5 %reduce-scatter.9.cloned.1.call-start = ((), (), s32[]{:S(2)}) async-start(), calls=%async_computation.9 | async-start | bytes 1228800 | tf_op jit(solution)/shard_map/reduce_scatter | solution.py:416
  847.6 139.0 %all-reduce.25.cloned.1.call-start = ((), (), s32[]{:S(2)}) async-start(), calls=%async_computation.16 | async-start | bytes 1966080 | tf_op jit(solution)/shard_map/psum | solution.py:112
  852.5 5.4 copy-start.2
  857.9 6.7 copy-start.86
  857.9 18.4 %copy-start.82 = (f32[240,320]{0,1:T(8,128)S(1)}, f32[240,320]{0,1:T(8,128)}, u32[]{:S(2)}) copy-start(f32[240,320]{0,1:T(8,128)} %param.35) | copy-start | bytes 921604
  877.7 51.8 %copy-start.73 = (f32[320,320]{1,0:T(8,128)S(1)}, f32[320,320]{1,0:T(8,128)}, u32[]{:S(2)}) copy-start(f32[320,320]{1,0:T(8,128)} %param.37) | copy-start | bytes 1228804
  931.9 14.0 %copy-start.76 = (f32[320,320]{1,0:T(8,128)S(1)}, f32[320,320]{1,0:T(8,128)}, u32[]{:S(2)}) copy-start(f32[320,320]{1,0:T(8,128)} %get-tuple-element.646) | copy-start | bytes 1228804
  949.8 38.4 %copy-start.83 = (f32[240,320]{0,1:T(8,128)S(1)}, f32[240,320]{0,1:T(8,128)}, u32[]{:S(2)}) copy-start(f32[240,320]{0,1:T(8,128)} %get-tuple-element.650) | copy-start | bytes 921604
  949.8 103.7 %all-reduce.23.cloned.1.call-start = ((), (), s32[]{:S(2)}) async-start(), calls=%async_computation.15 | async-start | bytes 1966080 | tf_op jit(solution)/shard_map/psum | solution.py:112
  999.5 102.5 %all-reduce.21.cloned.1.call-start = ((), (), s32[]{:S(2)}) async-start(), calls=%async_computation.14 | async-start | bytes 1966080 | tf_op jit(solution)/shard_map/psum | solution.py:112
  1001.3 7.8 copy-start.171
  1003.6 112.3 %collective-permute-start.2 = (bf16[1,1,20,20,320]{4,3,2,1,0:T(8,128)(2,1)}, bf16[1,1,20,20,320]{4,3,2,1,0:T(8,128)(2,1)}, u32[]{:S(2)}, u32[]{:S(2)}) collective-permute-start(bf16[1,1,20,20,320]{4,3,2,1,0:T(8,128)(2,1)} %get-tuple-element.669), channel_id=1, source_target_pairs={{0,1},{1,2},{2,3},{4,5},{5,6},{6,7},{8,9},{9,10},{10,11},{12,13},{... | collective-permute-start | bytes 768008 | tf_op jit(solution)/shard_map/ppermute | solution.py:29
  1007.0 108.9 %collective-permute-start.3 = (bf16[1,1,20,20,320]{4,3,2,1,0:T(8,128)(2,1)}, bf16[1,1,20,20,320]{4,3,2,1,0:T(8,128)(2,1)}, u32[]{:S(2)}, u32[]{:S(2)}) collective-permute-start(bf16[1,1,20,20,320]{4,3,2,1,0:T(8,128)(2,1)} %get-tuple-element.670), channel_id=1, source_target_pairs={{1,0},{2,1},{3,2},{5,4},{6,5},{7,6},{9,8},{10,9},{11,10},{13,12},{... | collective-permute-start | bytes 768008 | tf_op jit(solution)/shard_map/ppermute | solution.py:32
  1066.3 85.1 %all-reduce.19.cloned.1.call-start = ((), (), s32[]{:S(2)}) async-start(), calls=%async_computation.13 | async-start | bytes 1966080 | tf_op jit(solution)/shard_map/psum | solution.py:112
  1114.9 86.9 %all-reduce.17.cloned.1.call-start = ((), (), s32[]{:S(2)}) async-start(), calls=%async_computation.12 | async-start | bytes 1966080 | tf_op jit(solution)/shard_map/psum | solution.py:112
  1174.4 28.9 %copy-start.27 = (f32[240,320]{0,1:T(8,128)S(1)}, f32[240,320]{0,1:T(8,128)}, u32[]{:S(2)}) copy-start(f32[240,320]{0,1:T(8,128)} %copy-done.26) | copy-start | bytes 921604
  1174.4 28.9 %copy-start.50 = (f32[240,320]{0,1:T(8,128)S(1)}, f32[240,320]{0,1:T(8,128)}, u32[]{:S(2)}) copy-start(f32[240,320]{0,1:T(8,128)} %param.31) | copy-start | bytes 921604
  (169 other events, 376.1 us)
Sparse Core Ops, SparseCore 0:
  832.0 17.5 reduce-scatter.6
  852.2 23.0 reduce-scatter.12
  877.9 24.4 reduce-scatter.10
  905.0 24.4 reduce-scatter.8
  949.9 36.7 all-reduce.24
  999.6 38.7 all-reduce.22
  1066.5 35.5 all-reduce.20
  1115.1 36.3 all-reduce.18
  1165.4 36.3 all-reduce.16
where the time goes:
time: 1230 us; the launch traced here: 1220 us
  blocking collectives  358 us (29%)
  matrix products  305 us (25%)
  waiting for transfers between devices  223 us (18%)
  other arithmetic  155 us (13%)
  local copies, waits for them, and re-layouts  125 us (10%)
  starting transfers between devices  31.4 us (3%)
  between operations  20.8 us (2%)
    psum x1, blocking collectives, per_device(): summed_full = lax.psum((grad_qkv, grad_proj, grad_up, grad_down), 'clip')  227 us
    psum x5, waiting for transfers between devices, gram_sums(): lax.psum(self_product(blocks[0]).astype(jnp.bfloat16), 'frame')  125 us
    dot_general x20, matrix products, slot_scores(): jnp.einsum('cqd,ckd->cqk', query_block, slot_keys, preferred_element_type...  75.1 us
    convert_element_type x10, other arithmetic, block_backward(): grad_scores = (attn_probs * (grad_probs - row_dot)).astype(jnp.bfloat16)  67.7 us
    psum x1, blocking collectives, per_device(): lax.psum((vector_grad, up_bias_grad, kernel_grad), ('clip', 'frame'))  44.3 us
    dot_general x10, matrix products, block_backward(): jnp.einsum('cqk,cqd->ckd', attn_probs.astype(jnp.bfloat16), grad_block, p...  42.8 us
    all_gather x1, blocking collectives, per_device(): lax.all_gather(proj_weight.astype(jnp.bfloat16), 'frame', axis=0, tiled=T...  41.1 us
    dot_general x20, matrix products, self_product(): return jnp.dot(block_in.T, block_in, precision=HIGHEST)  35 us
  transfers between devices with their start and end apart: 17, of which 9 were waited for; matrix products, arithmetic and copies ran while one was open for 8% of the time, Pallas kernels for 0%

commit v1 on v0

v1 whole, which is shorter than its diff:
```python
import functools
import math

import jax
import jax.numpy as jnp
import numpy as np
from jax import lax
from jax.experimental import pallas as pl
from jax.experimental.pallas import tpu as pltpu
from jax.sharding import PartitionSpec as P

D = 320
HEADS = 5
HEAD_DIM = 64
PAIR = 2 * HEAD_DIM
WIDE = HEADS * PAIR
FF = 1280
NS_STEPS = 5
STEP = 10
CLIP_TOK = 3200
SHARE = 320

POLY_ONE = 3.4445
POLY_TWO = -4.775
POLY_THREE = 2.0315
LOG2E = math.log2(math.e)
SCORE_SCALE = HEAD_DIM**-0.5
MASKED = -1e30
MESH = pl.DeviceIdType.MESH
BF = jnp.bfloat16
F32 = jnp.float32
NT = (((1,), (1,)), ((), ()))
VMEM_SPEC = pl.BlockSpec(memory_space=pltpu.VMEM)


def dot_nt(left, right):
    return lax.dot_general(left, right, NT, preferred_element_type=F32)


def dot_nn(left, right):
    return jnp.dot(left, right, preferred_element_type=F32)


def lanes_of(rows):
    return lax.broadcasted_iota(jnp.int32, (rows, PAIR), 1)


CELL_AT = np.stack([np.arange(400) // 20, np.arange(400) % 20], axis=1).astype(np.float32)


def select_lanes(upper):
    row = lax.broadcasted_iota(jnp.int32, (D, WIDE), 0)
    col = lax.broadcasted_iota(jnp.int32, (D, WIDE), 1)
    source = lax.shift_left(lax.shift_right_logical(col, 7), 6) + (col & (HEAD_DIM - 1))
    half = col & HEAD_DIM
    return (source == row) & (half == (HEAD_DIM if upper else 0))


def flatten_frame(read_row, dst, base):
    for row in range(20):
        dst[base + 20 * row : base + 20 * row + 20, :] = read_row(row).astype(F32)


def build_slabs(center, edged, slot, flat, cells):
    blank = jnp.zeros((20, D), F32)
    edged[1, slot, 0:20, :] = blank
    edged[1, slot, 420:440, :] = blank
    edged[1, slot, 20:420, :] = flat
    center[1, slot] = flat
    col = cells[:, 1:2]
    for e, keep in ((0, col > 0.5), (2, col < 18.5)):
        moved = jnp.where(keep, edged[1, slot, 19 + e : 419 + e, :], 0.0)
        center[e, slot] = moved
        edged[e, slot, 0:20, :] = blank
        edged[e, slot, 420:440, :] = blank
        edged[e, slot, 20:420, :] = moved


def slab(center, edged, slot, b, e, start, size):
    if b == 1:
        return center[e, slot, pl.ds(start, size), :]
    return edged[e, slot, pl.ds(start + 20 * b, size), :]


def inside_of(side_ref, cells):
    side = side_ref[0].astype(F32) - 0.5
    return (cells[:, 0:1] < side) & (cells[:, 1:2] < side)


def norm_parts(rows):
    average = jnp.sum(rows, axis=-1, keepdims=True) * (1.0 / D)
    centered = rows - average
    variance = jnp.sum(centered * centered, axis=-1, keepdims=True) * (1.0 / D)
    scale = lax.rsqrt(variance + 1e-05)
    return centered * scale, scale


def frame_peers():
    f = lax.axis_index("frame")
    near = f + 1 - 2 * lax.rem(f, 2)
    across = lax.rem(f + 2, 4)
    return f, near, across, lax.rem(near + 2, 4)


def share_rows(rows, clips):
    return 16 * (-(-rows // (16 * clips)))


def greet_all(clips):
    barrier = pltpu.get_barrier_semaphore()
    for peer in frame_peers()[1:]:
        pl.semaphore_signal(barrier, inc=1, device_id={"frame": peer}, device_id_type=MESH)
    c = lax.axis_index("clip")

    def greet(step, carry):
        pl.semaphore_signal(
            barrier, inc=1, device_id={"clip": lax.rem(c + step, clips)}, device_id_type=MESH
        )
        return carry

    lax.fori_loop(1, clips, greet, 0)


def await_greetings(count):
    pl.semaphore_wait(pltpu.get_barrier_semaphore(), count)


def send(src, dst, send_sem, recv_sem, peer):
    return pltpu.make_async_remote_copy(
        src_ref=src,
        dst_ref=dst,
        send_sem=send_sem,
        recv_sem=recv_sem,
        device_id={"frame": peer},
        device_id_type=MESH,
    )


def halo_copies(first, last, halo, sems):
    f = lax.axis_index("frame")
    down = send(first, halo.at[1], sems.at[0, 0], sems.at[1, 0], jnp.maximum(f - 1, 0))
    up = send(last, halo.at[0], sems.at[0, 1], sems.at[1, 1], jnp.minimum(f + 1, 3))
    return down, up


def start_halos(down, up, halo):
    f = lax.axis_index("frame")

    @pl.when(f > 0)
    def _():
        down.start()

    @pl.when(f < 3)
    def _():
        up.start()

    @pl.when(f == 0)
    def _():
        halo[0] = jnp.zeros(halo.shape[1:], halo.dtype)

    @pl.when(f == 3)
    def _():
        halo[1] = jnp.zeros(halo.shape[1:], halo.dtype)


def wait_halos(down, up):
    f = lax.axis_index("frame")

    @pl.when(f > 0)
    def _():
        down.wait_send()
        up.wait_recv()

    @pl.when(f < 3)
    def _():
        up.wait_send()
        down.wait_recv()


EXP_SCALE = SCORE_SCALE * LOG2E


def tail_lanes(inside, copies):
    lane = lax.broadcasted_iota(jnp.int32, (inside.shape[0], PAIR), 1)
    tail = jnp.where(
        lane == HEAD_DIM,
        jnp.where(inside, 0.0, MASKED),
        jnp.where((lane > HEAD_DIM) & (lane < HEAD_DIM + 4), 1.0, 0.0),
    )
    return jnp.concatenate([tail] * copies, axis=0).astype(BF)


def front_kernel(
    clips,
    x_ref,
    side_ref,
    cells_ref,
    qkv_ref,
    proj_ref,
    up_ref,
    down_ref,
    vec_ref,
    taps_ref,
    tok_out,
    nhome_out,
    ncross_out,
    q_out,
    home_out,
    cross_out,
    kept_out,
    att_out,
    wq_out,
    wkv_out,
    others_out,
    tok_ref,
    nhome_ref,
    ncross_ref,
    q_ref,
    home_ref,
    cross_ref,
    kept_ref,
    att_ref,
    wq_ref,
    wkv_ref,
    others_ref,
    halo_ref,
    raw,
    outer,
    center,
    edged,
    qkv_full,
    tail,
    halo_sems,
    qkv_sems,
    other_sems,
    spread_sems,
    near_sems,
    cross_sems,
    out_sems,
):
    leaving = []

    def leave(src, dst):
        copy = pltpu.make_async_copy(src, dst, out_sems.at[len(leaving)])
        copy.start()
        leaving.append(copy)

    f, near, across, far = frame_peers()
    c = lax.axis_index("clip")
    greet_all(clips)
    part_rows = qkv_ref.shape[1]

    def qkv_rows(owner):
        return qkv_full.at[pl.ds(pl.multiple_of(owner * part_rows, 16), part_rows), :]

    qkv_full[pl.ds(pl.multiple_of(f * part_rows, 16), part_rows), :] = qkv_ref[...].T.astype(BF)
    start = 0
    for shard in (proj_ref, up_ref, down_ref):
        size = shard.shape[0]
        others_ref[f, start : start + size, :] = shard[...].astype(BF)
        start += size
    spare = others_ref.shape[1] - start
    if spare:
        others_ref[f, start : start + spare, :] = jnp.zeros((spare, D), BF)
    cells = cells_ref[...]
    inside = inside_of(side_ref, cells)
    for t in range(2):
        flatten_frame(lambda row, t=t: x_ref[0, t, row], raw, 400 * t)

    await_greetings(3 + clips - 1)
    down, up = halo_copies(x_ref.at[0, 0], x_ref.at[0, 1], halo_ref, halo_sems)
    start_halos(down, up, halo_ref)
    qkv_cross = send(qkv_rows(f), qkv_rows(f), qkv_sems.at[0, 1], qkv_sems.at[1, 1], across)
    qkv_near = send(qkv_rows(f), qkv_rows(f), qkv_sems.at[0, 0], qkv_sems.at[1, 0], near)
    qkv_relay = send(
        qkv_rows(across), qkv_rows(across), qkv_sems.at[0, 2], qkv_sems.at[1, 2], near
    )
    qkv_cross.start()
    qkv_near.start()

    part = others_ref.shape[1] // clips

    def part_of(owner, clip):
        return others_ref.at[owner, pl.ds(pl.multiple_of(clip * part, 16), part), :]

    other_near = send(
        others_ref.at[f], others_ref.at[f], other_sems.at[0, 0], other_sems.at[1, 0], near
    )
    other_cross = send(
        part_of(f, c), part_of(f, c), other_sems.at[0, 1], other_sems.at[1, 1], across
    )
    other_relay = send(
        others_ref.at[across],
        others_ref.at[across],
        other_sems.at[0, 2],
        other_sems.at[1, 2],
        near,
    )

    def spread(clip, landing):
        return pltpu.make_async_remote_copy(
            src_ref=part_of(across, c),
            dst_ref=part_of(across, landing),
            send_sem=spread_sems.at[0, clip],
            recv_sem=spread_sems.at[1, landing],
            device_id={"clip": clip},
            device_id_type=MESH,
        )

    def other_clips(act):
        def body(step, carry):
            act(lax.rem(c + step, clips))
            return carry

        lax.fori_loop(1, clips, body, 0)

    other_cross.start()
    other_near.start()

    for t in range(2):
        build_slabs(
            center, edged, t + 1, jnp.where(inside, raw[400 * t : 400 * t + 400, :], 0.0), cells
        )

    def conv_part(t, depths, start, total):
        for a in depths:
            for b in range(3):
                for e in range(3):
                    offset = 9 * a + 3 * b + e
                    total = total + taps_ref[offset : offset + 1, :] * slab(
                        center, edged, t + a, b, e, start, 40
                    )
        return total

    for t, depths in ((0, (1, 2)), (1, (0, 1))):

        def own_part(step, carry, t=t, depths=depths):
            start = pl.multiple_of(step * 40, 8)
            at = pl.ds(pl.multiple_of(start + 400 * t, 8), 40)
            tok_ref[at, :] = conv_part(t, depths, start, raw[at, :] + vec_ref[4:5, :])
            return carry

        lax.fori_loop(0, 10, own_part, 0)
    other_cross.wait_recv()
    other_clips(lambda clip: spread(clip, c).start())
    qkv_cross.wait_recv()
    qkv_relay.start()
    wait_halos(down, up)
    for side, slot in ((0, 0), (1, 3)):
        flatten_frame(lambda row, side=side: halo_ref[side, row], outer, 0)
        build_slabs(center, edged, slot, jnp.where(inside, outer[...], 0.0), cells)
    for t, depths in ((0, (0,)), (1, (2,))):

        def rim_part(step, carry, t=t, depths=depths):
            start = pl.multiple_of(step * 40, 8)
            at = pl.ds(pl.multiple_of(start + 400 * t, 8), 40)
            rows = conv_part(t, depths, start, tok_ref[at, :])
            tok_ref[at, :] = rows
            raw[at, :] = norm_parts(rows)[0] * vec_ref[0:1, :] + vec_ref[1:2, :]
            return carry

        lax.fori_loop(0, 10, rim_part, 0)
    rows = tok_ref.shape[0]
    nhome_ref[0:rows, :] = raw[...].astype(BF)

    piece = rows // HEADS

    def cross_copy(k):
        at = pl.ds(pl.multiple_of(k * piece, 16), piece)
        return send(
            nhome_ref.at[at, :],
            ncross_ref.at[at, :],
            cross_sems.at[0, 0, k],
            cross_sems.at[1, 0, k],
            across,
        )

    def relay_copy(k):
        return send(
            ncross_ref.at[pl.ds(pl.multiple_of(k * piece, 16), piece), :],
            ncross_ref.at[pl.ds(pl.multiple_of(rows + k * piece, 16), piece), :],
            cross_sems.at[0, 1, k],
            cross_sems.at[1, 1, k],
            near,
        )

    near_copy = send(
        nhome_ref.at[pl.ds(0, rows), :],
        nhome_ref.at[pl.ds(rows, rows), :],
        near_sems.at[0],
        near_sems.at[1],
        near,
    )
    for k in range(HEADS):
        cross_copy(k).start()
    near_copy.start()

    blank = jnp.zeros((1, HEAD_DIM), F32)

    def head_bias(row, h):
        return vec_ref[row : row + 1, HEAD_DIM * h : HEAD_DIM * (h + 1)]

    qkv_near.wait_recv()
    qkv_relay.wait_recv()
    for h in range(HEADS):
        wq_ref[PAIR * h : PAIR * h + HEAD_DIM, :] = qkv_full[HEAD_DIM * h : HEAD_DIM * (h + 1), :]
        wq_ref[PAIR * h + HEAD_DIM : PAIR * (h + 1), :] = jnp.zeros((HEAD_DIM, D), BF)
        wkv_ref[PAIR * h : PAIR * h + HEAD_DIM, :] = qkv_full[
            D + HEAD_DIM * h : D + HEAD_DIM * (h + 1), :
        ]
        wkv_ref[PAIR * h + HEAD_DIM : PAIR * (h + 1), :] = qkv_full[
            2 * D + HEAD_DIM * h : 2 * D + HEAD_DIM * (h + 1), :
        ]
    leave(tok_ref, tok_out)
    leave(wq_ref, wq_out)
    leave(wkv_ref, wkv_out)
    wide_query = jnp.concatenate(
        [part for h in range(HEADS) for part in (head_bias(5, h), blank)], axis=1
    )
    wide_pair = jnp.concatenate(
        [part for h in range(HEADS) for part in (blank, head_bias(6, h))], axis=1
    )

    def project(normed, weight, bias, place):
        joined = (dot_nt(normed, weight[...]) + bias).astype(BF)
        for h in range(HEADS):
            place(h, joined[:, PAIR * h : PAIR * (h + 1)])

    def place_query(h, value):
        q_ref[h] = value

    def place_own(h, value):
        home_ref[h, 0:rows, :] = value

    def place_near(h, value):
        home_ref[h, rows : 2 * rows, :] = value

    def place_cross(h, value):
        cross_ref[h] = value

    project(nhome_ref[0:rows, :], wq_ref, wide_query, place_query)
    project(nhome_ref[0:rows, :], wkv_ref, wide_pair, place_own)
    leave(q_ref, q_out)
    tail[...] = tail_lanes(inside, 4)
    tile = rows // 2
    mask_lane = jnp.where(lanes_of(tile) == HEAD_DIM, 1.0, 0.0).astype(BF)

    def tile_pass(t, source, last):
        at = pl.ds(pl.multiple_of(t * tile, 16), tile)
        lane = lanes_of(tile)
        for h in range(HEADS):
            keys = jnp.concatenate([source[h], tail[...]], axis=1)
            score = dot_nt(jnp.concatenate([q_ref[h, at, :], mask_lane], axis=1), keys)
            peak = jnp.max(score, axis=-1, keepdims=True)
            if last:
                kept = kept_ref[h, at, :]
                old_peak = kept[:, 0:1]
                peak = jnp.maximum(peak, old_peak)
            terms = jnp.exp2((score - peak) * EXP_SCALE).astype(BF)
            mixed = dot_nn(terms, keys)
            total = mixed[:, PAIR + HEAD_DIM + 1 : PAIR + HEAD_DIM + 2]
            mixed = mixed[:, 0:PAIR]
            if last:
                fade = jnp.exp2((old_peak - peak) * EXP_SCALE)
                total = total + fade * kept[:, 32:33]
                mixed = (mixed + fade * kept) / total
                log_sum = peak + jnp.log2(total) * (1.0 / EXP_SCALE)
                kept_ref[h, at, :] = jnp.where(lane < HEAD_DIM, log_sum, mixed)
                att_ref[h, at, :] = jnp.where(lane < HEAD_DIM, 0.0, mixed).astype(BF)
            else:
                kept_ref[h, at, :] = jnp.where(
                    lane < 32, peak, jnp.where(lane < HEAD_DIM, total, mixed)
                )

    def pass_on(k):
        cross_copy(k).wait_recv()
        relay_copy(k).start()

    def first_pass(t, carry):
        tile_pass(t, home_ref, False)

        @pl.when(t == 0)
        def _():
            for k in (0, 1, 2):
                pass_on(k)

        return carry

    def second_pass(t, carry):
        tile_pass(t, cross_ref, True)

        @pl.when(t == 0)
        def _():
            other_clips(lambda clip: spread(clip, clip).wait_recv())
            other_relay.start()

        return carry

    near_copy.wait_recv()
    leave(nhome_ref, nhome_out)
    project(nhome_ref[rows : 2 * rows, :], wkv_ref, wide_pair, place_near)
    leave(home_ref, home_out)
    lax.fori_loop(0, 2, first_pass, 0)
    for k in (3, 4):
        pass_on(k)
    for k in range(HEADS):
        relay_copy(k).wait_recv()
    leave(ncross_ref, ncross_out)
    project(ncross_ref[...], wkv_ref, wide_pair, place_cross)
    leave(cross_ref, cross_out)
    lax.fori_loop(0, 2, second_pass, 0)
    leave(kept_ref, kept_out)
    leave(att_ref, att_out)
    other_near.wait()
    other_relay.wait()
    leave(others_ref, others_out)
    other_clips(lambda clip: spread(clip, c).wait_send())
    for copy in (other_cross, near_copy, qkv_cross, qkv_near, qkv_relay):
        copy.wait_send()
    for k in range(HEADS):
        cross_copy(k).wait_send()
        relay_copy(k).wait_send()
    for copy in leaving:
        copy.wait()


def front(clips_in, clip_side, qkv, proj, up, down, vectors, taps, clips, collective_id):
    rows = 800
    other_rows = clips * share_rows(proj.shape[0] + up.shape[0] + down.shape[0], clips)
    outs = (
        ((rows, D), F32),
        ((2 * rows, D), BF),
        ((2 * rows, D), BF),
        ((HEADS, rows, PAIR), BF),
        ((HEADS, 2 * rows, PAIR), BF),
        ((HEADS, 2 * rows, PAIR), BF),
        ((HEADS, rows, PAIR), F32),
        ((HEADS, rows, PAIR), BF),
        ((WIDE, D), BF),
        ((WIDE, D), BF),
        ((4, other_rows, D), BF),
    )
    return pl.pallas_call(
        functools.partial(front_kernel, clips),
        in_specs=[VMEM_SPEC, pl.BlockSpec(memory_space=pltpu.SMEM)] + [VMEM_SPEC] * 7,
        out_specs=[pl.BlockSpec(memory_space=pl.ANY)] * len(outs),
        out_shape=[jax.ShapeDtypeStruct(*out) for out in outs],
        scratch_shapes=[pltpu.VMEM(*out) for out in outs]
        + [
            pltpu.VMEM((2, 20, 20, D), BF),
            pltpu.VMEM((rows, D), F32),
            pltpu.VMEM((400, D), F32),
            pltpu.VMEM((3, 4, 400, D), F32),
            pltpu.VMEM((3, 4, 440, D), F32),
            pltpu.VMEM((3 * D, D), BF),
            pltpu.VMEM((2 * rows, PAIR), BF),
            pltpu.SemaphoreType.DMA((2, 2)),
            pltpu.SemaphoreType.DMA((2, 3)),
            pltpu.SemaphoreType.DMA((2, 3)),
            pltpu.SemaphoreType.DMA((2, clips)),
            pltpu.SemaphoreType.DMA((2,)),
            pltpu.SemaphoreType.DMA((2, 2, HEADS)),
            pltpu.SemaphoreType.DMA((len(outs),)),
        ],
        compiler_params=pltpu.CompilerParams(
            collective_id=collective_id, has_side_effects=True, vmem_limit_bytes=60 * 2**20
        ),
        cost_estimate=pl.CostEstimate(
            flops=2**34, bytes_accessed=16 * 2**20, transcendentals=2**23
        ),
    )(clips_in, clip_side, jnp.asarray(CELL_AT), qkv, proj, up, down, vectors, taps)


INV_SQRT2 = math.sqrt(0.5)
INV_SQRT_2PI = 1.0 / math.sqrt(2.0 * math.pi)


def dot_tn(left, right):
    return lax.dot_general(left, right, (((0,), (0,)), ((), ())), preferred_element_type=F32)


def norm_back(upstream, unit, scale, gain):
    through = upstream * gain
    mean_one = jnp.sum(through, axis=-1, keepdims=True) * (1.0 / D)
    mean_two = jnp.sum(through * unit, axis=-1, keepdims=True) * (1.0 / D)
    return scale * (through - mean_one - unit * mean_two)


def column_sum(rows):
    return jnp.sum(rows, axis=0, keepdims=True)


def mid_kernel(
    att_ref,
    tok_ref,
    og_ref,
    side_ref,
    cells_ref,
    vec_ref,
    ubias_ref,
    others_ref,
    out_ref,
    gsec_ref,
    dout_ref,
    grads_ref,
    vsum_ref,
    raw,
    wide,
    act,
    ghid,
    normed,
    top,
    branch_low,
    att_low,
    proj_ref,
    up_ref,
    down_ref,
):
    start = 0
    for full in (proj_ref, up_ref, down_ref):
        size = full.shape[0] // 4
        for owner in range(4):
            full[size * owner : size * (owner + 1), :] = others_ref[owner, start : start + size, :]
        start += size
    inside = inside_of(side_ref, cells_ref[...])
    pick = select_lanes(True).astype(F32).astype(BF)
    wide[...] = dot_nn(proj_ref[...], pick).astype(BF)
    vsum_ref[...] = jnp.zeros(vsum_ref.shape, F32)
    for t in range(2):
        at = slice(400 * t, 400 * t + 400)
        heads = jnp.concatenate([att_ref[h, at, :] for h in range(HEADS)], axis=1)
        att_low[at, :] = dot_nt(heads, pick).astype(BF)
        second = tok_ref[at, :] + (dot_nt(heads, wide[...]) + vec_ref[7:8, :])
        unit, scale = norm_parts(second)
        normed_two = (unit * vec_ref[2:3, :] + vec_ref[3:4, :]).astype(BF)
        normed[at, :] = normed_two
        flatten_frame(lambda row, t=t: og_ref[0, t, row], raw, 0)
        grad_top = jnp.where(inside, raw[...], 0.0)
        top_low = grad_top.astype(BF)
        top[at, :] = top_low
        hidden = dot_nt(normed_two, up_ref[...]) + ubias_ref[...]
        half = 0.5 + 0.5 * lax.erf(hidden * INV_SQRT2)
        activated = (hidden * half).astype(BF)
        act[at, :] = activated
        slope = half + hidden * (INV_SQRT_2PI * jnp.exp(-0.5 * hidden * hidden))
        grad_hidden = (dot_nt(top_low, down_ref[...]) * slope).astype(BF)
        ghid[at, :] = grad_hidden
        raw[...] = second + (dot_nn(activated, down_ref[...]) + vec_ref[8:9, :])
        for row in range(20):
            out_ref[0, t, row] = raw[20 * row : 20 * row + 20, :].astype(BF)
        upstream = dot_nn(grad_hidden, up_ref[...])
        grad_second = grad_top + norm_back(upstream, unit, scale, vec_ref[2:3, :])
        gsec_ref[at, :] = grad_second
        low = grad_second.astype(BF)
        branch_low[at, :] = low
        dout = dot_nn(low, wide[...]).astype(BF)
        for h in range(HEADS):
            dout_ref[h, at, :] = dout[:, PAIR * h : PAIR * (h + 1)]
        vsum_ref[0:1, :] += column_sum(upstream * unit)
        vsum_ref[1:2, :] += column_sum(upstream)
        vsum_ref[2:3, :] += column_sum(low.astype(F32))
        vsum_ref[3:4, :] += column_sum(grad_top)
        bias_sum = column_sum(grad_hidden.astype(F32))
        for part in range(4):
            vsum_ref[4 + part : 5 + part, :] += bias_sum[:, D * part : D * (part + 1)]
    rows = up_ref.shape[0] // 4
    proj_rows = D // 4
    grad = dot_tn(branch_low[...], att_low[...]).astype(BF)
    for owner in range(4):
        grads_ref[owner, 0:proj_rows, :] = grad[proj_rows * owner : proj_rows * (owner + 1), :]
    for owner in range(4):
        at = slice(rows * owner, rows * (owner + 1))
        start = proj_rows
        grads_ref[owner, start : start + rows, :] = dot_tn(ghid[:, at], normed[...]).astype(BF)
        start = proj_rows + rows
        grads_ref[owner, start : start + rows, :] = dot_tn(act[:, at], top[...]).astype(BF)


def middle(attended, tokens, out_grad, clip_side, vectors, up_bias, others):
    rows = 800
    low = lambda *shape: jax.ShapeDtypeStruct(shape, BF)
    wide = lambda *shape: jax.ShapeDtypeStruct(shape, F32)
    return pl.pallas_call(
        mid_kernel,
        in_specs=[VMEM_SPEC] * 3 + [pl.BlockSpec(memory_space=pltpu.SMEM)] + [VMEM_SPEC] * 4,
        out_specs=[VMEM_SPEC] * 5,
        out_shape=[
            low(*out_grad.shape),
            wide(rows, D),
            low(HEADS, rows, PAIR),
            low(4, (D + 2 * FF) // 4, D),
            wide(8, D),
        ],
        scratch_shapes=[
            pltpu.VMEM((400, D), F32),
            pltpu.VMEM((D, WIDE), BF),
            pltpu.VMEM((rows, FF), BF),
            pltpu.VMEM((rows, FF), BF),
            pltpu.VMEM((rows, D), BF),
            pltpu.VMEM((rows, D), BF),
            pltpu.VMEM((rows, D), BF),
            pltpu.VMEM((rows, D), BF),
            pltpu.VMEM((D, D), BF),
            pltpu.VMEM((FF, D), BF),
            pltpu.VMEM((FF, D), BF),
        ],
        compiler_params=pltpu.CompilerParams(vmem_limit_bytes=56 * 2**20),
        cost_estimate=pl.CostEstimate(
            flops=6 * 2**30, bytes_accessed=12 * 2**20, transcendentals=2**21
        ),
    )(attended, tokens, out_grad, clip_side, jnp.asarray(CELL_AT), vectors, up_bias, others)


class RowSums:
    def __init__(self, clips, g_ref, at, pair_in, cross_out, cross_in, shares, shares_in, sums,
                 frame_sems, part_sems, sum_sems):
        self.clips = clips
        self.g = g_ref
        self.at = at
        self.pair_in = pair_in
        self.cross_out = cross_out
        self.cross_in = cross_in
        self.shares = shares
        self.shares_in = shares_in
        self.sums = sums
        self.part_sems = part_sems
        self.sum_sems = sum_sems
        f, near, across, far = frame_peers()
        self.f, self.across = f, across
        self.c = lax.axis_index("clip")
        sem = frame_sems
        part = lambda owner: g_ref.at[owner, pl.ds(at.start, at.stop - at.start), :]
        self.first = send(part(far), pair_in.at[0], sem.at[0, 0], sem.at[1, 0], near)
        self.second = send(part(near), pair_in.at[1], sem.at[0, 1], sem.at[1, 1], near)
        self.cross = send(cross_out, cross_in, sem.at[0, 2], sem.at[1, 2], across)

    def peer(self, step):
        return lax.rem(self.c + step, self.clips)

    def part_copy(self, step):
        return pltpu.make_async_remote_copy(
            src_ref=self.shares.at[self.peer(step)],
            dst_ref=self.shares_in.at[step],
            send_sem=self.part_sems.at[0, step],
            recv_sem=self.part_sems.at[1, step],
            device_id={"clip": self.peer(step)},
            device_id_type=MESH,
        )

    def sum_copy(self, step):
        return pltpu.make_async_remote_copy(
            src_ref=self.sums.at[self.c],
            dst_ref=self.sums.at[self.c],
            send_sem=self.sum_sems.at[0, step],
            recv_sem=self.sum_sems.at[1, step],
            device_id={"clip": self.peer(step)},
            device_id_type=MESH,
        )

    def each(self, act):
        def body(step, carry):
            act(step)
            return carry

        lax.fori_loop(1, self.clips, body, 0)

    def pair_step(self):
        self.first.start()
        self.second.start()

    def cross_step(self):
        self.first.wait()
        self.cross_out[...] = (
            self.g[self.across, self.at, :].astype(F32) + self.pair_in[0].astype(F32)
        ).astype(BF)
        self.cross.start()

    def share_step(self):
        self.second.wait()
        self.cross.wait()
        mine = (
            self.g[self.f, self.at, :].astype(F32)
            + self.pair_in[1].astype(F32)
            + self.cross_in[...].astype(F32)
        ).astype(BF)
        rows, chunk = mine.shape[0], self.shares.shape[1]
        spare = self.clips * chunk - rows
        if spare:
            mine = jnp.concatenate([mine, jnp.zeros((spare, D), BF)], axis=0)
        self.shares[...] = mine.reshape(self.clips, chunk, D)
        self.each(lambda step: self.part_copy(step).start())

    def sum_step(self):
        self.each(lambda step: self.part_copy(step).wait())

        def add_part(step, total):
            return total + self.shares_in[step].astype(F32)

        total = lax.fori_loop(1, self.clips, add_part, self.shares[self.c].astype(F32))
        self.sums[self.c] = total.astype(BF)
        self.each(lambda step: self.sum_copy(step).start())

    def finish(self):
        self.each(lambda step: self.sum_copy(step).wait())


def row_sums_scratch(rows, clips):
    chunk = share_rows(rows, clips)
    return [
        pltpu.VMEM((2, rows, D), BF),
        pltpu.VMEM((rows, D), BF),
        pltpu.VMEM((rows, D), BF),
        pltpu.VMEM((clips, chunk, D), BF),
        pltpu.VMEM((clips, chunk, D), BF),
        pltpu.VMEM((clips, chunk, D), BF),
        pltpu.SemaphoreType.DMA((2, 3)),
        pltpu.SemaphoreType.DMA((2, clips)),
        pltpu.SemaphoreType.DMA((2, clips)),
    ]


EARLY_PARTS = (slice(0, 400), slice(400, 720))


def row_pieces(start, size, block):
    pieces, skip = [], 0
    while skip < size:
        owner, row = divmod(start + skip, block)
        step = min(size - skip, block - row)
        pieces.append((owner, row, skip, step))
        skip += step
    return pieces


def back_kernel(
    clips,
    q_ref,
    dout_ref,
    kept_ref,
    cross_ref,
    home_in,
    nhome_in,
    ncross_in,
    wq_in,
    wkv_in,
    side_ref,
    cells_ref,
    early_ref,
    gnorm_ref,
    own_ref,
    out_ref,
    bsum_ref,
    one_ref,
    two_ref,
    home_ref,
    nhome_ref,
    ncross_ref,
    wq_ref,
    wkv_ref,
    grads_ref,
    grads_in,
    extra,
    qd_t,
    tail,
    low_one,
    low_two,
    low_three,
    dq_sum,
    dq_low,
    turned_pairs,
    pair_grad,
    dnormed,
    pair_out,
    pair_in,
    cross_out,
    cross_in,
    pair_sems,
    cross_sems,
    late_sems,
    grad_sems,
    *sum_refs,
):
    f, near, across, far = frame_peers()
    rows = q_ref.shape[1]
    greet_all(clips)
    late = [
        pltpu.make_async_copy(src, dst, late_sems.at[k])
        for k, (src, dst) in enumerate(
            (
                (ncross_in, ncross_ref),
                (wkv_in, wkv_ref),
                (home_in, home_ref),
                (nhome_in, nhome_ref),
                (wq_in, wq_ref),
            )
        )
    ]
    for copy in late:
        copy.start()
    half = len(sum_refs) // 2
    one = RowSums(clips, early_ref, EARLY_PARTS[0], *sum_refs[:half])
    two = RowSums(clips, early_ref, EARLY_PARTS[1], *sum_refs[half:])
    tail[...] = tail_lanes(inside_of(side_ref, cells_ref[...]), 4)
    await_greetings(3 + clips - 1)
    one.pair_step()
    two.pair_step()
    lower = lax.broadcasted_iota(jnp.int32, (PAIR, 1), 0) < HEAD_DIM
    scale_of = jnp.where(lower, SCORE_SCALE, 1.0)
    chunks = ((0, 512, low_one), (512, 512, low_two), (1024, 576, low_three))

    def minus_parts(column, lane):
        high = column.astype(BF).astype(F32)
        mid = (column - high).astype(BF).astype(F32)
        rest = column - high - mid
        return jnp.where(
            lane == HEAD_DIM + 1,
            -high,
            jnp.where(lane == HEAD_DIM + 2, -mid, jnp.where(lane == HEAD_DIM + 3, -rest, 0.0)),
        )

    def prepare(h):
        lane = lanes_of(rows)
        kept = kept_ref[h]
        queries, douts = q_ref[h].astype(F32), dout_ref[h].astype(F32)
        log_sum = kept[:, 0:1]
        row_dot = jnp.sum(douts * kept, axis=-1, keepdims=True)
        of_queries = jnp.where(lane == HEAD_DIM, 1.0, minus_parts(log_sum, lane))
        extra[h, 0:rows, :] = of_queries.astype(BF)
        extra[h, rows : 2 * rows, :] = minus_parts(row_dot, lane).astype(BF)
        qd_t[h] = jnp.concatenate([queries, douts], axis=0).T.astype(BF)
        bsum_ref[1, h] = column_sum(douts)

    def head_pass(h, source, add):
        pairs = source[h]
        both = jnp.concatenate([q_ref[h], dout_ref[h]], axis=0)
        both = jnp.concatenate([both, extra[h]], axis=1)
        products = [
            dot_nt(
                both,
                jnp.concatenate(
                    [pairs[start : start + size, :], tail[start : start + size, :]], axis=1
                ),
            )
            for start, size, low in chunks
        ]
        total = dq_sum[h] if add else None
        at = pl.ds(pl.multiple_of(h * PAIR, PAIR), PAIR)
        for (start, size, low), product in zip(chunks, products):
            probs = jnp.exp2(product[0:rows, :] * EXP_SCALE)
            low[0:rows, :] = (probs * product[rows : 2 * rows, :]).astype(BF)
            low[rows : 2 * rows, :] = probs.astype(BF)
            part = dot_nn(low[0:rows, :], pairs[start : start + size, :])
            total = part if total is None else total + part
            turned = dot_nn(qd_t[h], low[...]) * scale_of
            turned_pairs[at, start : start + size] = turned.astype(BF)
        if add:
            total = jnp.where(lanes_of(rows) < HEAD_DIM, total * SCORE_SCALE, 0.0)
            dq_low[h] = total.astype(BF)
            bsum_ref[0, h] = column_sum(total)
        else:
            dq_sum[h] = total

    def of_normed(normed, add):
        grad = dot_nn(turned_pairs[...], normed[...])
        pair_grad[...] = pair_grad[...] + grad if add else grad
        total = dot_nn(wkv_ref[...].astype(F32).T.astype(BF), turned_pairs[...]).T
        dnormed[...] = total[0:rows, :]
        pair_out[...] = total[rows : 2 * rows, :].astype(BF)

    def pair_copy(phase):
        return send(
            pair_out, pair_in.at[phase], pair_sems.at[0, phase], pair_sems.at[1, phase], near
        )

    to_across = send(cross_out, cross_in, cross_sems.at[0], cross_sems.at[1], across)

    def cross_pass(h, carry):
        prepare(h)
        head_pass(h, cross_ref, False)

        @pl.when(h == 0)
        def _():
            one.cross_step()
            two.cross_step()

        @pl.when(h == 3)
        def _():
            one.share_step()

        return carry

    def home_pass(h, carry):
        head_pass(h, home_ref, True)

        @pl.when(h == 0)
        def _():
            pair_copy(0).wait()
            cross_out[...] = (dnormed[...] + pair_in[0].astype(F32)).astype(BF)
            to_across.start()
            two.share_step()

        @pl.when(h == 1)
        def _():
            one.sum_step()

        @pl.when(h == 3)
        def _():
            two.sum_step()

        return carry

    lax.fori_loop(0, HEADS, cross_pass, 0)
    for copy in late:
        copy.wait()
    of_normed(ncross_ref, False)
    pair_copy(0).start()
    lax.fori_loop(0, HEADS, home_pass, 0)
    of_normed(nhome_ref, True)
    pair_copy(1).start()

    block = grads_ref.shape[1]

    def place(start, values):
        for owner, row, skip, size in row_pieces(start, values.shape[0], block):
            grads_ref[owner, row : row + size, :] = values[skip : skip + size, :]

    dq = jnp.concatenate([dq_low[h] for h in range(HEADS)], axis=1)
    of_queries = dot_tn(dq, nhome_ref[0:rows, :]).astype(BF)
    for h in range(HEADS):
        of_pairs = pair_grad[PAIR * h : PAIR * (h + 1), :].astype(BF)
        place(HEAD_DIM * h, of_queries[PAIR * h : PAIR * h + HEAD_DIM, :])
        place(D + HEAD_DIM * h, of_pairs[0:HEAD_DIM, :])
        place(2 * D + HEAD_DIM * h, of_pairs[HEAD_DIM:PAIR, :])
    to_pair = [
        send(grads_ref.at[peer], grads_in.at[k], grad_sems.at[0, k], grad_sems.at[1, k], near)
        for k, peer in enumerate((far, near))
    ]
    for copy in to_pair:
        copy.start()
    total = dnormed[...] + dot_nn(dq, wq_ref[...])
    to_across.wait()
    pair_copy(1).wait()
    gnorm_ref[...] = total + pair_in[1].astype(F32) + cross_in[...].astype(F32)
    one.finish()
    two.finish()
    for copy in to_pair:
        copy.wait()
    out_ref[...] = (grads_ref[across].astype(F32) + grads_in[0].astype(F32)).astype(BF)
    own_ref[...] = grads_ref[f].astype(F32) + grads_in[1].astype(F32)
    one_ref[...] = one.sums[...].reshape(one_ref.shape)
    two_ref[...] = two.sums[...].reshape(two_ref.shape)


def attention_back(operands, clips, collective_id):
    rows, block = 800, 3 * D // 4
    wide = lambda *shape: jax.ShapeDtypeStruct(shape, F32)
    low = lambda *shape: jax.ShapeDtypeStruct(shape, BF)
    parts = [part.stop - part.start for part in EARLY_PARTS]
    return pl.pallas_call(
        functools.partial(back_kernel, clips),
        in_specs=[VMEM_SPEC] * 4
        + [pl.BlockSpec(memory_space=pl.ANY)] * 5
        + [pl.BlockSpec(memory_space=pltpu.SMEM)]
        + [VMEM_SPEC] * 2,
        out_specs=[VMEM_SPEC] * 6,
        out_shape=[
            wide(rows, D),
            wide(block, D),
            low(block, D),
            wide(2, HEADS, 1, PAIR),
        ]
        + [low(clips * share_rows(part, clips), D) for part in parts],
        scratch_shapes=[
            pltpu.VMEM((HEADS, 2 * rows, PAIR), BF),
            pltpu.VMEM((2 * rows, D), BF),
            pltpu.VMEM((2 * rows, D), BF),
            pltpu.VMEM((WIDE, D), BF),
            pltpu.VMEM((WIDE, D), BF),
            pltpu.VMEM((4, block, D), BF),
            pltpu.VMEM((2, block, D), BF),
            pltpu.VMEM((HEADS, 2 * rows, PAIR), BF),
            pltpu.VMEM((HEADS, PAIR, 2 * rows), BF),
            pltpu.VMEM((2 * rows, PAIR), BF),
            pltpu.VMEM((2 * rows, 512), BF),
            pltpu.VMEM((2 * rows, 512), BF),
            pltpu.VMEM((2 * rows, 576), BF),
            pltpu.VMEM((HEADS, rows, PAIR), F32),
            pltpu.VMEM((HEADS, rows, PAIR), BF),
            pltpu.VMEM((WIDE, 2 * rows), BF),
            pltpu.VMEM((WIDE, D), F32),
            pltpu.VMEM((rows, D), F32),
            pltpu.VMEM((rows, D), BF),
            pltpu.VMEM((2, rows, D), BF),
            pltpu.VMEM((rows, D), BF),
            pltpu.VMEM((rows, D), BF),
            pltpu.SemaphoreType.DMA((2, 2)),
            pltpu.SemaphoreType.DMA((2,)),
            pltpu.SemaphoreType.DMA((5,)),
            pltpu.SemaphoreType.DMA((2, 2)),
        ]
        + row_sums_scratch(parts[0], clips)
        + row_sums_scratch(parts[1], clips),
        compiler_params=pltpu.CompilerParams(
            collective_id=collective_id, has_side_effects=True, vmem_limit_bytes=62 * 2**20
        ),
        cost_estimate=pl.CostEstimate(
            flops=2**35, bytes_accessed=24 * 2**20, transcendentals=2**24
        ),
    )(*operands)


def newton_schulz(whole):
    wide = whole.astype(F32)
    norm = jnp.sqrt(jnp.sum(wide * wide)) + 1e-07
    eye = (
        lax.broadcasted_iota(jnp.int32, (D, D), 0) == lax.broadcasted_iota(jnp.int32, (D, D), 1)
    ).astype(F32)
    turned = dot_nt(eye.astype(BF), whole) / norm

    def iterate(step, current):
        held = current.astype(BF)
        gram = dot_nt(held, held)
        gram_low = gram.astype(BF)
        poly = POLY_TWO * gram + POLY_THREE * dot_nn(gram_low, gram_low)
        return POLY_ONE * current + dot_nn(poly.astype(BF), held)

    return lax.fori_loop(0, NS_STEPS, iterate, turned)


OWNER_OF = (3, 1, 0, 2)
QKV_AT = OWNER_OF[0]


def tail_kernel(
    clips,
    gnorm_ref,
    own_ref,
    across_ref,
    bsum_ref,
    tok_ref,
    gsec_ref,
    x_ref,
    side_ref,
    cells_ref,
    taps_ref,
    vec_ref,
    mid_sums_ref,
    one_ref,
    two_ref,
    qkv_m_ref,
    proj_m_ref,
    up_m_ref,
    down_m_ref,
    ingrad_ref,
    late_ref,
    scaled_ref,
    vsum_ref,
    cross_in,
    shares,
    shares_in,
    old_rows,
    new_rows,
    new_low,
    first,
    first_low,
    rim,
    outer,
    center,
    edged,
    v_mine,
    v_frames,
    v_total,
    v_clips,
    low,
    gathered,
    grad_sems,
    part_sems,
    row_sems,
    spread_sems,
    rim_sems,
    vf_sems,
    vc_sems,
    there_sems,
    back_sems,
):
    f, near, across, far = frame_peers()
    c = lax.axis_index("clip")
    block = own_ref.shape[0]
    owners, chunk = shares.shape[0], shares.shape[1]

    def each(count, act):
        def body(step, carry):
            act(step)
            return carry

        lax.fori_loop(0, count, body, 0)

    def other_clips(act):
        each(clips - 1, lambda step: act(lax.rem(c + 1 + step, clips)))

    @pl.when(f == QKV_AT)
    def _():
        gathered[:, owners * chunk : SHARE, :] = jnp.zeros((4, SHARE - owners * chunk, D), BF)

    proj_rows = proj_m_ref.shape[0]

    @pl.when(f == OWNER_OF[1])
    def _():
        gathered[:, proj_rows:SHARE, :] = jnp.zeros((4, SHARE - proj_rows, D), BF)

    greet_all(clips)
    barrier = pltpu.get_barrier_semaphore()

    def greet(clip, frame):
        pl.semaphore_signal(
            barrier, inc=1, device_id={"clip": clip, "frame": frame}, device_id_type=MESH
        )

    @pl.when(f == QKV_AT)
    def _():
        for step in (1, 2, 3):
            other_clips(lambda clip, step=step: greet(clip, (QKV_AT + step) % 4))

    @pl.when(f != QKV_AT)
    def _():
        other_clips(lambda clip: greet(clip, QKV_AT))

    down, up = halo_copies(first_low.at[0], first_low.at[1], rim, rim_sems)

    @pl.when(f == QKV_AT)
    def _():
        await_greetings(3 + 4 * (clips - 1))

    @pl.when(f != QKV_AT)
    def _():
        await_greetings(3 + 2 * (clips - 1))

    to_across = send(across_ref, cross_in, grad_sems.at[0], grad_sems.at[1], across)
    to_across.start()

    upstream = gnorm_ref[...]
    unit, scale = norm_parts(tok_ref[...])
    grad_first = gsec_ref[...] + norm_back(upstream, unit, scale, vec_ref[0:1, :])
    first[...] = grad_first
    first_low[...] = grad_first.astype(BF).reshape(first_low.shape)
    start_halos(down, up, rim)

    moments = (None, proj_m_ref, up_m_ref, down_m_ref)

    def to_owner(which):
        at = pl.ds(0, moments[which].shape[0])
        return send(
            low.at[which, at, :],
            gathered.at[f, at, :],
            there_sems.at[0, which],
            there_sems.at[1, f],
            OWNER_OF[which],
        )

    for which in (3, 2, 1):
        rows = moments[which].shape[0]
        summed = one_ref[80:400, :] if which == 2 else (two_ref if which == 3 else one_ref)[0:rows, :]
        low[which, 0:rows, :] = (0.95 * moments[which][...] + summed.astype(F32)).astype(BF)

        @pl.when(f != OWNER_OF[which])
        def _(which=which):
            to_owner(which).start()

    old_rows[0:block, :] = qkv_m_ref[...].T
    if owners * chunk > block:
        old_rows[block : owners * chunk, :] = jnp.zeros((owners * chunk - block, D), F32)

    v_mine[0:1, :] = column_sum(upstream * unit)
    v_mine[1:2, :] = column_sum(upstream)
    v_mine[2:4, :] = mid_sums_ref[0:2, :]
    v_mine[4:5, :] = column_sum(grad_first)
    v_mine[5:6, :] = jnp.concatenate(
        [bsum_ref[0, h, :, 0:HEAD_DIM] for h in range(HEADS)], axis=1
    )
    v_mine[6:7, :] = jnp.concatenate(
        [bsum_ref[1, h, :, HEAD_DIM:PAIR] for h in range(HEADS)], axis=1
    )
    v_mine[7:9, :] = mid_sums_ref[2:4, :]
    v_mine[9:13, :] = mid_sums_ref[4:8, :]

    cells = cells_ref[...]
    inside = inside_of(side_ref, cells)
    for t in range(2):
        build_slabs(center, edged, t + 1, first[400 * t : 400 * t + 400, :], cells)

    def part_copy(owner):
        return pltpu.make_async_remote_copy(
            src_ref=shares.at[owner],
            dst_ref=shares_in.at[c],
            send_sem=part_sems.at[0, owner],
            recv_sem=part_sems.at[1, c],
            device_id={"clip": owner},
            device_id_type=MESH,
        )

    def other_owners(act):
        def step(owner):
            @pl.when(owner != c)
            def _():
                act(owner)

        each(owners, step)

    to_across.wait()
    mine = (own_ref[...] + cross_in[...].astype(F32)).astype(BF)
    if owners * chunk > block:
        mine = jnp.concatenate([mine, jnp.zeros((owners * chunk - block, D), BF)], axis=0)
    shares[...] = mine.reshape(owners, chunk, D)
    other_owners(lambda owner: part_copy(owner).start())

    wait_halos(down, up)
    for side, slot in ((0, 0), (1, 3)):
        build_slabs(center, edged, slot, rim[side].astype(F32), cells)

    def row_copy(clip):
        return pltpu.make_async_remote_copy(
            src_ref=new_rows.at[c],
            dst_ref=new_rows.at[c],
            send_sem=row_sems.at[0, clip],
            recv_sem=row_sems.at[1, c],
            device_id={"clip": clip},
            device_id_type=MESH,
        )

    def spread_copy(clip):
        return pltpu.make_async_remote_copy(
            src_ref=new_low,
            dst_ref=gathered.at[f, pl.ds(pl.multiple_of(c * chunk, 16), chunk), :],
            send_sem=spread_sems.at[4, clip],
            recv_sem=spread_sems.at[f, c],
            device_id={"clip": clip, "frame": QKV_AT},
            device_id_type=MESH,
        )

    def share_sum():
        @pl.when(c < owners)
        def _():
            shares_in[c] = shares[c]

            def arrive(clip):
                pltpu.make_async_remote_copy(
                    src_ref=shares.at[0],
                    dst_ref=shares_in.at[clip],
                    send_sem=part_sems.at[0, 0],
                    recv_sem=part_sems.at[1, clip],
                    device_id={"clip": clip},
                    device_id_type=MESH,
                ).wait_recv()

            other_clips(arrive)

            def add_part(clip, total):
                return total + shares_in[clip].astype(F32)

            total = lax.fori_loop(0, clips, add_part, jnp.zeros((chunk, D), F32))
            at = pl.ds(pl.multiple_of(c * chunk, 16), chunk)
            fresh = 0.95 * old_rows[at, :] + total
            new_rows[c] = fresh
            new_low[...] = fresh.astype(BF)
            other_clips(lambda clip: spread_copy(clip).start())

            @pl.when(f != QKV_AT)
            def _():
                spread_copy(c).start()

            @pl.when(f == QKV_AT)
            def _():
                gathered[QKV_AT, at, :] = new_low[...]

            other_clips(lambda clip: row_copy(clip).start())

    for t in range(2):
        flatten_frame(lambda row, t=t: x_ref[0, t, row], outer, 0)
        outer[...] = jnp.where(inside, outer[...], 0.0)
        for a in range(3):

            def plane(step, totals, t=t, a=a):
                start = pl.multiple_of(step * 16, 16)
                at = pl.ds(pl.multiple_of(start + 400 * t, 16), 16)
                masked = outer[pl.ds(start, 16), :]
                total = jnp.zeros((16, D), F32)
                sums_out = []
                for b in range(3):
                    for e in range(3):
                        offset = 9 * a + 3 * b + e
                        piece = slab(center, edged, t + 2 - a, 2 - b, 2 - e, start, 16)
                        total = total + taps_ref[offset : offset + 1, :] * piece
                        product = masked * piece
                        sums_out.append(totals[3 * b + e] + (product[0:8, :] + product[8:16, :]))
                if a == 0:
                    ingrad_ref[at, :] = total
                else:
                    ingrad_ref[at, :] += total
                return tuple(sums_out)

            totals = lax.fori_loop(0, 25, plane, tuple(jnp.zeros((8, D), F32) for _ in range(9)))
            for which, total in enumerate(totals):
                at = slice(13 + 9 * a + which, 14 + 9 * a + which)
                if t == 0:
                    v_mine[at, :] = column_sum(total)
                else:
                    v_mine[at, :] += column_sum(total)
        at = slice(400 * t, 400 * t + 400)
        ingrad_ref[at, :] = first[at, :] + jnp.where(inside, ingrad_ref[at, :], 0.0)
        if t == 0:
            share_sum()

    v_copies = []
    for which, peer in enumerate((near, across, far)):
        copy = send(v_mine, v_frames.at[f], vf_sems.at[0, which], vf_sems.at[1, which], peer)
        copy.start()
        v_copies.append(copy)
    v_frames[f] = v_mine[...]

    @pl.when(f == QKV_AT)
    def _():
        def rows_arrive(frame, clip):
            pltpu.make_async_remote_copy(
                src_ref=new_low,
                dst_ref=gathered.at[frame, pl.ds(pl.multiple_of(clip * chunk, 16), chunk), :],
                send_sem=spread_sems.at[4, clip],
                recv_sem=spread_sems.at[frame, clip],
                device_id={"clip": clip, "frame": frame},
                device_id_type=MESH,
            ).wait_recv()

        other_owners(lambda clip: rows_arrive(QKV_AT, clip))
        for step in (1, 2, 3):
            frame = (QKV_AT + step) % 4
            each(owners, lambda clip, frame=frame: rows_arrive(frame, clip))

    for which in (1, 2, 3):

        @pl.when(f != OWNER_OF[which])
        def _(which=which):
            to_owner(which).wait_send()

        @pl.when(f == OWNER_OF[which])
        def _(which=which):
            at = pl.ds(0, moments[which].shape[0])
            gathered[OWNER_OF[which], at, :] = low[which, at, :]
            for other in range(4):
                if other != OWNER_OF[which]:
                    send(
                        low.at[0, at, :],
                        gathered.at[other, at, :],
                        there_sems.at[0, 0],
                        there_sems.at[1, other],
                        other,
                    ).wait_recv()

    turned = newton_schulz(gathered[...].reshape(4 * SHARE, D))
    low[...] = turned.T.astype(BF).reshape(low.shape)
    row_counts = (block, *(ref.shape[0] for ref in moments[1:]))

    def back_copy(which, step):
        at = pl.ds(0, row_counts[which])
        to = (OWNER_OF[which] + step) % 4
        return send(
            low.at[to, at, :],
            scaled_ref.at[which, at, :],
            back_sems.at[0, step],
            back_sems.at[1, which],
            to,
        )

    for which in range(4):

        @pl.when(f == OWNER_OF[which])
        def _(which=which):
            for step in (2, 1, 3):
                back_copy(which, step).start()
            at = pl.ds(0, row_counts[which])
            scaled_ref[which, at, :] = low[OWNER_OF[which], at, :]

    for copy in v_copies:
        copy.wait()
    v_total[...] = v_frames[0] + v_frames[1] + v_frames[2] + v_frames[3]

    def v_copy(clip):
        return pltpu.make_async_remote_copy(
            src_ref=v_total,
            dst_ref=v_clips.at[c],
            send_sem=vc_sems.at[0, clip],
            recv_sem=vc_sems.at[1, c],
            device_id={"clip": clip},
            device_id_type=MESH,
        )

    other_clips(lambda clip: v_copy(clip).start())
    v_clips[c] = v_total[...]

    other_owners(lambda owner: part_copy(owner).wait_send())

    @pl.when(c < owners)
    def _():
        other_clips(lambda clip: spread_copy(clip).wait_send())

        @pl.when(f != QKV_AT)
        def _():
            spread_copy(c).wait_send()

        other_clips(lambda clip: row_copy(clip).wait_send())

    def new_rows_arrive(clip):
        pltpu.make_async_remote_copy(
            src_ref=new_rows.at[0],
            dst_ref=new_rows.at[clip],
            send_sem=row_sems.at[0, 0],
            recv_sem=row_sems.at[1, clip],
            device_id={"clip": clip},
            device_id_type=MESH,
        ).wait_recv()

    other_owners(new_rows_arrive)
    late_ref[...] = new_rows[...].reshape(late_ref.shape)

    def v_arrives(clip):
        v_copy(clip).wait_send()
        pltpu.make_async_remote_copy(
            src_ref=v_total,
            dst_ref=v_clips.at[clip],
            send_sem=vc_sems.at[0, clip],
            recv_sem=vc_sems.at[1, clip],
            device_id={"clip": clip},
            device_id_type=MESH,
        ).wait_recv()

    other_clips(v_arrives)

    def add_v(step, total):
        return total + v_clips[step]

    vsum_ref[...] = lax.fori_loop(0, clips, add_v, jnp.zeros(vsum_ref.shape, F32))
    for which in range(4):

        @pl.when(f == OWNER_OF[which])
        def _(which=which):
            for step in (2, 1, 3):
                back_copy(which, step).wait_send()

        @pl.when(f != OWNER_OF[which])
        def _(which=which):
            back_copy(which, 1).wait_recv()


def tail_part(operands, clips, qkv_rows, collective_id):
    rows = 800
    chunk = share_rows(qkv_rows, clips)
    owners = -(-qkv_rows // chunk)
    vector_shape = (40, D)
    vmem = pltpu.VMEM
    dma = pltpu.SemaphoreType.DMA
    return pl.pallas_call(
        functools.partial(tail_kernel, clips),
        in_specs=[VMEM_SPEC] * 7 + [pl.BlockSpec(memory_space=pltpu.SMEM)] + [VMEM_SPEC] * 10,
        out_specs=[VMEM_SPEC] * 4,
        out_shape=[
            jax.ShapeDtypeStruct((rows, D), F32),
            jax.ShapeDtypeStruct((owners * chunk, D), F32),
            jax.ShapeDtypeStruct((4, SHARE, D), BF),
            jax.ShapeDtypeStruct(vector_shape, F32),
        ],
        scratch_shapes=[
            vmem((qkv_rows, D), BF),
            vmem((owners, chunk, D), BF),
            vmem((clips, chunk, D), BF),
            vmem((owners * chunk, D), F32),
            vmem((owners, chunk, D), F32),
            vmem((chunk, D), BF),
            vmem((rows, D), F32),
            vmem((2, 400, D), BF),
            vmem((2, 400, D), BF),
            vmem((400, D), F32),
            vmem((3, 4, 400, D), F32),
            vmem((3, 4, 440, D), F32),
            vmem(vector_shape, F32),
            vmem((4,) + vector_shape, F32),
            vmem(vector_shape, F32),
            vmem((clips,) + vector_shape, F32),
            vmem((4, SHARE, D), BF),
            vmem((4, SHARE, D), BF),
            dma((2,)),
            dma((2, clips)),
            dma((2, clips)),
            dma((5, clips)),
            dma((2, 2)),
            dma((2, 3)),
            dma((2, clips)),
            dma((2, 4)),
            dma((2, 4)),
        ],
        compiler_params=pltpu.CompilerParams(
            collective_id=collective_id, has_side_effects=True, vmem_limit_bytes=60 * 2**20
        ),
        cost_estimate=pl.CostEstimate(
            flops=2**33, bytes_accessed=16 * 2**20, transcendentals=2**20
        ),
    )(*operands)


def adamw(param, mean_old, square_old, gradient, rate_value, decay):
    mean_new = 0.9 * mean_old + 0.1 * gradient
    square_new = 0.999 * square_old + 0.001 * gradient * gradient
    mean_hat = mean_new / (1.0 - 0.9**STEP)
    square_hat = square_new / (1.0 - 0.999**STEP)
    return (
        mean_new,
        square_new,
        param - rate_value * (mean_hat / (jnp.sqrt(square_hat) + 1e-08) + decay * param),
    )


RATES = (0.2 * math.sqrt(3.0), 0.12 * math.sqrt(CLIP_TOK), 0.2 * math.sqrt(FF / D), 0.2)


def update_kernel(*refs):
    ingrad_ref, late_ref, one_ref, two_ref, scaled_ref, vsum_ref = refs[:6]
    weights, moments, vectors, taps = refs[6:10], refs[10:13], refs[13:16], refs[16:19]
    out_ref, new_moments, new_weights = refs[19], refs[20:24], refs[24:28]
    new_vectors, new_taps = refs[28:31], refs[31:34]
    for t in range(2):
        for row in range(20):
            at = 400 * t + 20 * row
            out_ref[0, t, row] = ingrad_ref[at : at + 20, :]
    rows = weights[0].shape[1]
    new_moments[0][...] = late_ref[0:rows, :].T
    new_weights[0][...] = 0.999 * weights[0][...] - RATES[0] * (
        scaled_ref[0, 0:rows, :].astype(F32).T
    )
    for which in (1, 2, 3):
        rows = weights[which].shape[0]
        summed = one_ref[80:400, :] if which == 2 else (two_ref if which == 3 else one_ref)[0:rows, :]
        new_moments[which][...] = 0.95 * moments[which - 1][...] + summed.astype(F32)
        new_weights[which][...] = 0.999 * weights[which][...] - RATES[which] * scaled_ref[
            which, 0:rows, :
        ].astype(F32)
    for (param, mean, square), outs, at, rate, decay in (
        (vectors, new_vectors, slice(0, 9), 0.2, 0.0),
        (taps, new_taps, slice(13, 40), 0.05, 0.01),
    ):
        for ref, value in zip(
            outs, adamw(param[...], mean[...], square[...], vsum_ref[at, :], rate, decay)
        ):
            ref[...] = value


def update(ingrad, late, one, two, scaled, vector_sums, weights, moments, vectors, taps, grid_shape):
    operands = [ingrad, late, one, two, scaled, vector_sums, *weights, *moments[1:], *vectors, *taps]
    outs = [jax.ShapeDtypeStruct(grid_shape, F32)]
    outs += [jax.ShapeDtypeStruct(x.shape, F32) for x in (*moments, *weights, *vectors, *taps)]
    return pl.pallas_call(
        update_kernel,
        in_specs=[VMEM_SPEC] * len(operands),
        out_specs=[VMEM_SPEC] * len(outs),
        out_shape=outs,
        compiler_params=pltpu.CompilerParams(vmem_limit_bytes=62 * 2**20),
        cost_estimate=pl.CostEstimate(
            flops=2**22, bytes_accessed=12 * 2**20, transcendentals=2**14
        ),
    )(*operands)


def per_device(
    clips_in,
    out_grad,
    clip_side,
    qkv_weight,
    proj_weight,
    up_weight,
    down_weight,
    qkv_moment,
    proj_moment,
    up_moment,
    down_moment,
    vectors,
    vector_mean,
    vector_square,
    up_bias,
    up_bias_mean,
    up_bias_square,
    conv_kernel,
    kernel_mean,
    kernel_square,
):
    clips = lax.axis_size("clip")
    weights = (qkv_weight, proj_weight, up_weight, down_weight)
    moments = (qkv_moment, proj_moment, up_moment, down_moment)
    (
        tokens,
        normed_home,
        normed_cross,
        heads_q,
        home,
        cross,
        kept,
        heads_out,
        query_weight,
        pair_weight,
        other_weights,
    ) = front(clips_in, clip_side, qkv_weight.T, *weights[1:], vectors, conv_kernel, clips, 0)
    block_out, grad_second, douts, early_grads, mid_sums = middle(
        heads_out,
        tokens,
        out_grad,
        clip_side,
        vectors,
        up_bias.reshape(1, FF),
        other_weights,
    )
    grad_normed, qkv_own, qkv_out, bias_sums, sums_one, sums_two = attention_back(
        (
            heads_q,
            douts,
            kept,
            cross,
            home,
            normed_home,
            normed_cross,
            query_weight,
            pair_weight,
            clip_side,
            jnp.asarray(CELL_AT),
            early_grads,
        ),
        clips,
        1,
    )
    ingrad, late_moment, scaled, vector_sums = tail_part(
        (
            grad_normed,
            qkv_own,
            qkv_out,
            bias_sums,
            tokens,
            grad_second,
            clips_in,
            clip_side,
            jnp.asarray(CELL_AT),
            conv_kernel,
            vectors,
            mid_sums,
            sums_one,
            sums_two,
            qkv_moment.T,
            *moments[1:],
        ),
        clips,
        qkv_weight.shape[0],
        2,
    )
    updated = update(
        ingrad,
        late_moment,
        sums_one,
        sums_two,
        scaled,
        vector_sums,
        (qkv_weight.T, *weights[1:]),
        (qkv_moment.T, *moments[1:]),
        (vectors, vector_mean, vector_square),
        (conv_kernel, kernel_mean, kernel_square),
        clips_in.shape,
    )
    input_grad = updated[0]
    new_moments = (updated[1].T, *updated[2:5])
    new_weights = (updated[5].T, *updated[6:9])
    bias_new = adamw(
        up_bias, up_bias_mean, up_bias_square, vector_sums[9:13].reshape(FF), 0.2, 0.0
    )
    outs = [block_out, input_grad]
    for moment, weight in zip(new_moments, new_weights):
        outs += [moment, weight]
    return (*outs, *updated[9:12], *bias_new, *updated[12:15])


def solution(mesh):
    big = P("clip", "frame", None, None, None)
    rows = P("frame", None)
    return jax.shard_map(
        per_device,
        mesh=mesh,
        in_specs=(big, big, P("clip")) + (rows,) * 8 + (P(),) * 9,
        out_specs=(big, big) + (rows,) * 8 + (P(),) * 9,
        check_vma=False,
    )
```

time: 1230 us -> 210 us (0.17)
  blocking collectives: 358 us -> 0 us
  matrix products: 305 us -> 0 us
  waiting for transfers between devices: 223 us -> 0 us
  Pallas kernels: 0 us -> 195 us
  other arithmetic: 155 us -> 0.62 us
  local copies, waits for them, and re-layouts: 125 us -> 9.78 us
  starting transfers between devices: 31.4 us -> 0 us
  between operations: 20.8 us -> 1.6 us
    dot_general x146 -> x0, matrix products: 305 us -> none  [the longest x20 75.1 us: slot_scores(): jnp.einsum('cqd,ckd->cqk', query_block, slot_keys, preferred_element_type...]
    psum x3 -> x0, blocking collectives: 278 us -> none  [the longest x1 227 us: per_device(): summed_full = lax.psum((grad_qkv, grad_proj, grad_up, grad_down), 'clip')]
    pallas_call x0 -> x5, Pallas kernels: none -> 195 us  [the longest x1 67.2 us: front(): pl.pallas_call(functools.partial(front_kernel, clips), in_specs=[VMEM_SPE...]
    psum x5 -> x0, waiting for transfers between devices: 125 us -> none  [gram_sums(): lax.psum(self_product(blocks[0]).astype(jnp.bfloat16), 'frame')]
    all_gather x4 -> x0, blocking collectives: 80.5 us -> none  [the longest x1 41.1 us: per_device(): lax.all_gather(proj_weight.astype(jnp.bfloat16), 'frame', axis=0, tiled=T...]
    convert_element_type x18 -> x0, other arithmetic: 72.6 us -> none  [the longest x10 67.7 us: block_backward(): grad_scores = (attn_probs * (grad_probs - row_dot)).astype(jnp.bfloat16)]
    reduce_scatter x3 -> x0, waiting for transfers between devices: 49.2 us -> none  [the longest x1 24.7 us: per_device(): lax.psum_scatter(summed_full[3].astype(jnp.bfloat16), 'frame', scatter_di...]
    reduce_sum x25 -> x0, other arithmetic: 43.2 us -> none  [the longest x10 12.6 us: block_forward(): totals = jnp.sum(exp_terms, axis=-1, keepdims=True)]
  transfers between devices with their start and end apart: 17 -> 0, of which waited for: 9 -> 0; matrix products, arithmetic and copies ran while one was open for 8% -> 0% of each run, Pallas kernels for 0% -> 0%
where the time goes in v1:
time: 210 us; the launch traced here: 207 us
  Pallas kernels  195 us (93%)
  local copies, waits for them, and re-layouts  9.78 us (5%)
    pallas_call x1, Pallas kernels, front(): pl.pallas_call(functools.partial(front_kernel, clips), in_specs=[VMEM_SPE...  67.2 us
    pallas_call x1, Pallas kernels, tail_part(): pl.pallas_call(functools.partial(tail_kernel, clips), in_specs=[VMEM_SPEC...  54.8 us
    pallas_call x1, Pallas kernels, attention_back(): pl.pallas_call(functools.partial(back_kernel, clips), in_specs=[VMEM_SPEC...  52.2 us
    pallas_call x1, Pallas kernels, middle(): pl.pallas_call(mid_kernel, in_specs=[VMEM_SPEC] * 3 + [pl.BlockSpec(memor...  15.6 us
    unnamed x14, local copies, waits for them, and re-layouts  7.69 us
    pallas_call x1, Pallas kernels, update(): pl.pallas_call(update_kernel, in_specs=[VMEM_SPEC] * len(operands), out_s...  4.99 us

profile of v1, /device:TPU:1, one launch (start us, length us, event | category | flops | bytes accessed | tf_op | source)
XLA Modules:
  0.0 206.9 jit_solution(13835628695595219002)
XLA Ops:
  0.7 0.0 copy-start.1
  1.4 1.3 reshape.44.ubias_ref
  2.7 2.0 copy.40.x_ref
  4.7 0.0 copy-done.1
  4.7 1.0 copy.41.og_ref
  5.7 67.2 %shard_map.348 = (f32[800,320]{1,0:T(8,128)}, bf16[1600,320]{1,0:T(8,128)(2,1)}, bf16[1600,320]{1,0:T(8,128)(2,1)}, bf16[5,800,128]{2,1,0:T(8,128)(2,1)}, bf16[5...) custom-call(bf16[1,2,20,20,320]{4,3,2,1,0:T(8,128)(2,1)} %copy.40.x_, ...), custom_call_target="tpu_custom_call" | custom-call | flops 17179869184 | bytes 16777216 | tf_op jit(solution)/shard_map/pallas_call | solution.py:543
  73.0 15.6 %shard_map.349 = (bf16[1,2,20,20,320]{4,3,2,1,0:T(8,128)(2,1)}, f32[800,320]{1,0:T(8,128)}, bf16[5,800,128]{2,1,0:T(8,128)(2,1)}, bf16[4,720,320]{2,1,0:T(8,128)(2,1)}, f32[8,320]{1,0:T(8,128)}) custom-call(bf16[5,800,128]{2,1,0:T(8,128)(2,1)} %get-tuple-element.60.att_ref, f32[800,320]{1,0:T(8,128)} %get-tuple-element.61.tok_ref, ...), custom_call_target="tpu_custom_call" | custom-call | flops 6442450944 | bytes 12582912 | tf_op jit(solution)/shard_map/pallas_call | solution.py:683
  88.6 0.0 copy-start
  88.6 52.2 %shard_map.350 = (f32[800,320]{1,0:T(8,128)}, f32[240,320]{1,0:T(8,128)}, bf16[240,320]{1,0:T(8,128)(2,1)}, f32[2,5,1,128]{3,2,1,0:T(1,128)}, bf16[512,320]{1,0:T(8,128)(2,1)}, /*index=5*/bf16[384,320]{1,0:T(8,128)(2,1)}) custom-call(bf16[5,800,128]{2,1,0:T(8,128)(2,1)} %get-tuple-element.64.q_ref, bf16[5,800,128]{2,1,0:T(8,128)(2,1)} %get-tuple-element.65.dout_ref, ...), custom_call_target="tpu_custom_call" | custom-call | flops 34359738368 | bytes 25165824 | tf_op jit(solution)/shard_map/pallas_call | solution.py:1059
  140.8 0.0 copy-done
  140.8 1.3 copy.43
  142.1 0.0 copy-start.2
  142.1 0.0 copy-start.3
  142.1 0.0 copy-start.4
  142.1 54.8 %shard_map.351 = (f32[800,320]{1,0:T(8,128)}, f32[256,320]{1,0:T(8,128)}, bf16[4,320,320]{2,1,0:T(8,128)(2,1)}, f32[40,320]{1,0:T(8,128)}) custom-call(f32[800,320]{1,0:T(8,128)} %get-tuple-element.74.gnorm_ref, f32[240,320]{1,0:T(8,128)} %get-tuple-element.75.own_ref, bf16[240,320]{1,0:T(8,128)(2,1)} %get-tuple-element.76.across_ref, ...), custom_call_target="tpu_custom_call" | custom-call | flops 8589934592 | bytes 16777216 | tf_op jit(solution)/shard_map/pallas_call | solution.py:1559
  197.0 0.7 slice.3
  197.7 0.1 reshape.45
  197.8 0.0 copy-done.2
  197.8 0.0 copy-done.3
  197.8 0.0 copy-done.4
  197.8 0.6 multiply_subtract_fusion
  198.4 5.0 %shard_map.352 = (f32[1,2,20,20,320]{4,3,2,1,0:T(8,128)}, f32[320,240]{1,0:T(8,128)}, f32[80,320]{1,0:T(8,128)}, f32[320,320]{1,0:T(8,128)}, f32[320,320]{1,0:T(...) custom-call(f32[800,320]{1,0:T(8,128)} %get-tuple-element.82.refs_0_, ...), custom_call_target="tpu_custom_call" | custom-call | flops 4194304 | bytes 12582912 | tf_op jit(solution)/shard_map/pallas_call | solution.py:1657
  203.4 3.4 %copy.44 = f32[1,2,20,20,320]{4,1,3,2,0:T(2,128)} copy(f32[1,2,20,20,320]{4,3,2,1,0:T(8,128)} %get-tuple-element.102) | data formatting | bytes 2048000
Async XLA Ops:
  0.7 4.1 %copy-start.1 = (bf16[1,2,20,20,320]{4,1,3,2,0:T(2,128)(2,1)S(1)}, bf16[1,2,20,20,320]{4,1,3,2,0:T(2,128)(2,1)}, u32[]{:S(2)}) copy-start(bf16[1,2,20,20,320]{4,1,3,2,0:T(2,128)(2,1)} %param.22) | copy-start | bytes 1536004
  88.6 52.2 %copy-start = (bf16[1,2,20,20,320]{4,3,2,1,0:T(8,128)(2,1)S(1)}, bf16[1,2,20,20,320]{4,3,2,1,0:T(8,128)(2,1)}, u32[]{:S(2)}) copy-start(bf16[1,2,20,20,320]{4,3,2,1,0:T(8,128)(2,1)} %get-tuple-element.101) | copy-start | bytes 1536004
  142.1 55.6 %copy-start.2 = (f32[1280]{0:T(1024)S(1)}, f32[1280]{0:T(1024)}, u32[]{:S(2)}) copy-start(f32[1280]{0:T(1024)} %param.35) | copy-start | bytes 15364
  142.1 55.6 %copy-start.3 = (f32[1280]{0:T(1024)S(1)}, f32[1280]{0:T(1024)}, u32[]{:S(2)}) copy-start(f32[1280]{0:T(1024)} %param.37) | copy-start | bytes 15364
  142.1 55.6 %copy-start.4 = (f32[1280]{0:T(1024)S(1)}, f32[1280]{0:T(1024)}, u32[]{:S(2)}) copy-start(f32[1280]{0:T(1024)} %param.36) | copy-start | bytes 15364
